TPU v7x, 256 devices: a whole 4x4x8 slice. The times are simulated.
256 devices in a mesh: blk: 64 (over z, x, core), head: 4 (over y), sample: 1.
Axes of the slice: x: 4, y: 4, z: 8, core: 2. Of those that a mesh axis runs over, the one named last changes fastest.
Arguments:
- query_single: bfloat16 [1024, 384], P(('sample', 'blk')), may hold values from -6 to 6
- query_frames: float32 [12, 1024], P(None, ('sample', 'blk')), may hold values from -6 to 6, as said below
- query_chain: int32 [1024], P(('sample', 'blk')), may hold values from 0 to 23
- key_single: bfloat16 [12288, 384], P(('sample', 'blk')), may hold values from -6 to 6
- key_frames: float32 [12, 12288], P(None, ('sample', 'blk')), may hold values from -6 to 6, as said below
- key_chain: int32 [12288], P(('sample', 'blk')), may hold values from 0 to 23
- key_mask: int32 [12288], P(('sample', 'blk')), may hold values 0 or 1
- pair: bfloat16 [1024, 12288, 128], P(('sample', 'blk'), 'head'), may hold values from -1600 to 1600
- w_q: bfloat16 [384, 192], P(None, 'head'), may hold values from -0.3125 to 0.3125
- w_k: bfloat16 [384, 192], P(None, 'head'), may hold values from -0.3125 to 0.3125
- w_v: bfloat16 [384, 192], P(None, 'head'), may hold values from -0.3125 to 0.3125
- w_qp: bfloat16 [384, 144], P(None, 'head'), may hold values from -0.3125 to 0.3125
- w_kp: bfloat16 [384, 144], P(None, 'head'), may hold values from -0.3125 to 0.3125
- w_vp: bfloat16 [384, 288], P(None, 'head'), may hold values from -0.3125 to 0.3125
- w_bias: bfloat16 [128, 12], replicated, may hold values from -1 to 1
- head_weight: float32 [12], P('head'), may hold values from -1 to 2
- chain_bias: float32 [12], P('head'), may hold values from -2 to 2
- w_out: bfloat16 [2112, 384], replicated, may hold values from -0.25 to 0.25
- ln_gain: float32 [384], replicated, may hold values from 0.5 to 1.5
- w_frame: bfloat16 [384, 6], replicated, may hold values from -0.3125 to 0.3125
Outputs:
- single_out: bfloat16 [1024, 384], P(('sample', 'blk'))
- frames_out: float32 [12, 1024], P(None, ('sample', 'blk'))
Inputs may be any that keep to these rules, and one draw needn't show every extreme that they name: `query_frames`: the first nine rows are each residue's rotation matrix row after row, orthonormal with determinant one; the last three are its translation. `key_frames`: the first nine rows are each residue's rotation matrix row after row, orthonormal with determinant one; the last three are its translation.
All inputs are finite; a program needn't handle non-finite values. No bound on the sum of `key_mask` on one device may be relied on, other than what follows from the above.
Results may differ from a plain program's by a relative error of at most 0.009.
Values may be sent and summed in bfloat16 or wider, within the bound.
A program may use at most 128 MiB of HBM per device.

v0:
```python
import math

import jax
import jax.numpy as jnp
from jax import lax
from jax.experimental import pallas as pl
from jax.experimental.pallas import tpu as pltpu
from jax.sharding import PartitionSpec as P

F32 = jnp.float32
BF16 = jnp.bfloat16
HIGH = lax.Precision.HIGHEST
MESH = pl.DeviceIdType.MESH

HEADS = 12
QPTS = 4
ROWS = 192
GROUPS = 8
GROUP = 24
CHUNKS = 8
KEYS = 384
WEIGHT_L = math.sqrt(1.0 / 3.0)
WEIGHT_C = math.sqrt(2.0 / (9.0 * QPTS))

Z_IN, LEFT_IN, RIGHT_IN, HALF_LEFT_IN, HALF_RIGHT_IN, CORE_IN = 0, 2, 4, 6, 8, 10
ROWS_IN, WEIGHTS_IN, PART_IN, UPDATE_IN, META = 18, 21, 24, 27, 30
Z_OUT, Z_BACK, RIGHT_OUT, LEFT_OUT, HALF_RIGHT_OUT, HALF_LEFT_OUT, CORE_OUT = 0, 2, 3, 5, 7, 9, 11
ROWS_OUT, WEIGHTS_OUT, PART_OUT, UPDATE_OUT, META_OUT = 19, 22, 25, 28, 31


def iota(shape, dim):
    return lax.broadcasted_iota(jnp.int32, shape, dim)


def by3(v):
    return (v * 171) >> 9


def by12(v):
    return (v * 171) >> 11


def by24(v):
    return (v * 2731) >> 16


def by48(v):
    return (v * 1366) >> 16


def by80(v):
    return (v * 820) >> 16


def by96(v):
    return (v * 683) >> 16


def ones_where(cond, dtype=BF16):
    return jnp.where(cond, 1.0, 0.0).astype(dtype)


def mm(lhs, rhs, precision=None):
    return lax.dot_general(
        lhs, rhs, (((1,), (0,)), ((), ())), precision=precision, preferred_element_type=F32
    )


def nt(lhs, rhs, precision=None):
    return lax.dot_general(
        lhs, rhs, (((1,), (1,)), ((), ())), precision=precision, preferred_element_type=F32
    )


def short(v):
    return v.astype(BF16).astype(F32)


def split2(v):
    first = short(v)
    return first, short(v - first)


def split3(v):
    first = short(v)
    second = short(v - first)
    return first, second, short(v - first - second)


def head16(head):
    owner = by3(head)
    return owner * 4 + head - owner * 3


def quat_rotation(w, x, y, z):
    return [
        1.0 - 2.0 * (y * y + z * z),
        2.0 * (x * y - w * z),
        2.0 * (x * z + w * y),
        2.0 * (x * y + w * z),
        1.0 - 2.0 * (x * x + z * z),
        2.0 * (y * z - w * x),
        2.0 * (x * z - w * y),
        2.0 * (y * z + w * x),
        1.0 - 2.0 * (x * x + y * y),
    ]


def own_rows(single, meta, w_q, w_k, w_qp, head_weight, chain_bias):
    rows = 48
    row = iota((rows, 1), 0)
    query = by3(row)
    local_head = row - query * 3
    spread = query == iota((rows, 16), 1)
    single_rows = mm(ones_where(spread), single).astype(BF16)
    q_s = mm(single_rows, w_q).astype(BF16).astype(F32)
    col = iota((rows, 48), 1)
    q_s = jnp.where((col >> 4) == local_head, q_s, 0.0).astype(BF16)
    scalar = nt(q_s, w_k) * (WEIGHT_L / 4.0)

    frames = nt(ones_where(spread, F32), meta, HIGH)
    local = mm(single_rows, w_qp)
    col = iota((rows, 36), 1)
    local = jnp.where(by12(col) == local_head, local, 0.0)
    lane = iota((1, 128), 1)
    comp = jnp.where(lane < 12, lane, lane - 12)
    axis = comp >> 2
    point = comp & 3
    inside = lane < 24
    source = iota((36, 128), 0)
    source = source - by12(source) * 12
    entry = iota((16, 128), 0)
    placed = mm(frames, ones_where((entry == axis + 9) & inside, F32), HIGH)
    for b in range(3):
        here = mm(local, ones_where((source == point + 4 * b) & inside, F32), HIGH)
        turn = mm(frames, ones_where((entry == axis * 3 + b) & inside, F32), HIGH)
        placed = placed + turn * here
    norm = jnp.sum(jnp.where(lane < 12, placed * placed, 0.0), axis=1, keepdims=True)

    def per_head(ref):
        return jnp.where(local_head == 0, ref[0], jnp.where(local_head == 1, ref[1], ref[2]))

    weight = per_head(head_weight)
    soft = jnp.maximum(weight, 0.0) + jnp.log(1.0 + jnp.exp(-jnp.abs(weight)))
    coeff = soft * (WEIGHT_L * WEIGHT_C / 2.0)
    point_hi, point_lo = split2(2.0 * coeff * placed)
    chain_hi, chain_lo = split2(per_head(chain_bias) * WEIGHT_L)
    own_chain = frames[:, 12:13]
    lane_f = lane.astype(F32)
    compact = jnp.where(lane < 12, point_hi, jnp.where(inside, point_lo, 0.0))
    compact = jnp.where((lane >= 24) & (lane < 48) & (own_chain == lane_f - 24.0), chain_hi, compact)
    compact = jnp.where((lane >= 48) & (lane < 72) & (own_chain == lane_f - 48.0), chain_lo, compact)
    for first, values in ((72, split3(-coeff * norm)), (75, split3(coeff))):
        for step, value in enumerate(values):
            compact = jnp.where(lane == first + step, value, compact)
    return scalar.astype(BF16), compact.astype(BF16)


def own_weights(w_kp, w_v, w_vp):
    row = iota((48, 36), 0)
    col = iota((48, 36), 1)
    head = row & 3
    pick = (col == head * 12 + (row >> 4) * 4 + ((row >> 2) & 3)) & (head < 3)
    key_points = nt(ones_where(pick), w_kp).astype(BF16)
    values = nt(ones_where(iota((48, 48), 0) == iota((48, 48), 1)), w_v).astype(BF16)
    row = iota((80, 72), 0)
    col = iota((80, 72), 1)
    b = by24(row)
    rest = row - b * 24
    pick = (col == (rest >> 3) * 24 + b * 8 + (rest & 7)) & (row < 72)
    value_points = nt(ones_where(pick), w_vp).astype(BF16)
    return key_points, values, value_points


def all_rows(packs):
    shape = (ROWS, ROWS)
    row, col = iota(shape, 0), iota(shape, 1)
    query = by12(row)
    owner = by48(col)
    rest = col - owner * 48
    col_query = by3(rest)
    pick = (query == col_query) & (row - query * 12 == owner * 3 + rest - col_query * 3)
    rows = mm(ones_where(pick), packs).astype(BF16)
    compact = rows[:, 384:]
    lane = iota((1, 512), 1)
    again = jnp.where(lane < 192, lane, lane - 192)
    source = ((again >> 6) * 4 + ((again >> 4) & 3)) + jnp.where(lane < 192, 0, 12)
    source = jnp.where(lane >= 384, -1, source)
    source = jnp.where((lane >= 384) & (lane < 408), lane - 360, source)
    source = jnp.where((lane >= 416) & (lane < 440), lane - 368, source)
    source = jnp.where((lane >= 496) & (lane < 499), lane - 424, source)
    other = mm(compact, ones_where(iota((128, 512), 0) == source))
    row = iota((ROWS, 1), 0)
    place = head16(row - by12(row) * 12)
    mine = (lane & 15) == place
    other = jnp.where(mine | (lane >= 384), other, 0.0)
    other = jnp.where(mine & (lane >= 448) & (lane < 496), 1.0, other)
    spot, col = iota((16, ROWS), 0), iota((16, ROWS), 1)
    pick = (head16(col) == spot) & (col < 12)
    factors = mm(ones_where(pick), compact)
    factor = factors[:, 75:76] + factors[:, 76:77] + factors[:, 77:78]
    return rows[:, :384], other.astype(BF16), factor


def kernel(
    single_q, meta_q, single_k, meta_k, pair, w_q, w_k, w_v, w_qp, w_kp, w_vp, w_bias, w_out, gain, w_frame,
    head_weight, chain_bias,
    single_out, frames_out,
    v_single, v_meta, v_wq, v_wk, v_wv, v_wqp, v_wkp, v_wvp, v_wbias, v_wout, v_gain, v_wframe,
    pairs, keys, metas, bias, pack_rows, pack_weights,
    rows_single, rows_other, w_points, w_values, w_vpoints, factors, bias_rows,
    acc_pair, acc_single, acc_points, top, total,
    part_out, part_in, updates,
    local_sem, pair_sem, send_sem, recv_sem,
):
    y = lax.axis_index("head")
    blk = lax.axis_index("blk")
    z = lax.div(blk, 8)
    core = lax.rem(blk, 2)
    x = lax.rem(lax.div(blk, 2), 4)
    r = lax.rem(z - 2 * y + 8, 8)
    upper = (r >= 1) & (r <= 4)
    depth = jnp.where(upper, r - 1, lax.rem(8 - r, 8))
    step_z = jnp.where(upper, 1, -1)
    near = jnp.where(upper, 1, 0)

    def device(zz, xx, cc):
        return (zz * 4 + xx) * 2 + cc

    out_z = device(lax.rem(z + step_z + 8, 8), x, core)
    in_z = device(lax.rem(z - step_z + 8, 8), x, core)
    right = device(z, lax.rem(x + 1, 4), core)
    left = device(z, lax.rem(x + 3, 4), core)
    sibling = device(z, x, 1 - core)

    small = [
        (single_q, v_single), (meta_q, v_meta), (w_q, v_wq), (w_k, v_wk), (w_qp, v_wqp), (w_kp, v_wkp),
        (w_v, v_wv), (w_vp, v_wvp), (w_bias, v_wbias), (gain, v_gain), (w_frame, v_wframe),
        (w_out.at[pl.ds(pl.multiple_of(y * 528, 528), 528)], v_wout),
    ]
    small = [pltpu.make_async_copy(src, dst, local_sem.at[i]) for i, (src, dst) in enumerate(small)]

    def item(i):
        phase = 0 if i in (0, 1, 2, 6) else 1
        kind = i if i < 3 else (i - 3 if i < 6 else 3)
        plane = near if phase == 0 else 1 - near
        return phase, kind, plane * 4 + lax.rem(x + (0, 3, 1, 2)[kind], 4)

    own_index = item(0)[2]
    own_copies = [
        pltpu.make_async_copy(single_k, keys.at[own_index, core], local_sem.at[12]),
        pltpu.make_async_copy(meta_k, metas.at[own_index, core], local_sem.at[13]),
    ]
    pair_copies = [
        pltpu.make_async_copy(pair.at[pl.ds(2 * g, 2)], pairs.at[pl.ds(2 * g, 2)], pair_sem.at[g])
        for g in range(GROUPS)
    ]

    barrier = pltpu.get_barrier_semaphore()
    for other in (
        device(lax.rem(z + 1, 8), x, core), device(lax.rem(z + 7, 8), x, core), right, left, sibling
    ):
        pl.semaphore_signal(barrier, inc=1, device_id={"blk": other}, device_id_type=MESH)
    for step in (1, 2, 3):
        pl.semaphore_signal(
            barrier, inc=1, device_id={"head": lax.rem(y + step, 4)}, device_id_type=MESH
        )

    @pl.when(depth == 0)
    def _():
        for copy in own_copies:
            copy.start()

    for copy in small:
        copy.start()
    for copy in pair_copies:
        copy.start()

    def remote(src, dst, sent, received, target):
        return pltpu.make_async_remote_copy(
            src_ref=src, dst_ref=dst, send_sem=send_sem.at[sent], recv_sem=recv_sem.at[received],
            device_id=target, device_id_type=MESH,
        )

    def block(index, cc, sent, received, target, part=None, meta=True):
        ref = keys.at[index, cc]
        if part is not None:
            ref = keys.at[index, cc, pl.ds(96 * part, 96)]
        copies = [remote(ref, ref, sent, received, {"blk": target})]
        if meta:
            ref = metas.at[index, cc]
            copies.append(remote(ref, ref, sent + META_OUT, received + META, {"blk": target}))
        return copies

    def sends(i):
        phase, kind, index = item(i)
        result = []
        if kind == 0:
            result.append((depth < 3, block(index, core, Z_OUT + phase, Z_IN + phase, out_z)))
            if phase == 0:
                result.append((depth == 0, block(index, core, Z_BACK, Z_IN + 1, in_z)))
            result.append((None, block(index, core, RIGHT_OUT + phase, LEFT_IN + phase, right)))
            result.append((None, block(index, core, LEFT_OUT + phase, RIGHT_IN + phase, left)))
        if kind == 1:
            result.append((None, block(index, core, HALF_RIGHT_OUT + phase, HALF_LEFT_IN + phase, right, 0)))
        if kind == 2:
            result.append(
                (None, block(index, core, HALF_LEFT_OUT + phase, HALF_RIGHT_IN + phase, left, 1, False))
            )
        result.append((None, block(index, core, CORE_OUT + i, CORE_IN + i, sibling)))
        return result

    def run(condition, copies, verb):
        def act():
            for copy in copies:
                getattr(copy, verb)()

        if condition is None:
            act()
        else:
            pl.when(condition)(act)

    def event(i):
        phase, kind, index = item(i)
        if kind == 0:
            arriving = block(index, core, 0, Z_IN + phase, sibling)
            run(depth > 0 if phase == 0 else None, arriving, "wait_recv")
        elif kind == 3:
            first = block(index, core, 0, HALF_LEFT_IN + phase, sibling, 0)
            second = block(index, core, 0, HALF_RIGHT_IN + phase, sibling, 1, False)
            for copy in first + second:
                copy.wait_recv()
        else:
            place = (LEFT_IN, RIGHT_IN)[kind - 1] + phase
            for copy in block(index, core, 0, place, sibling):
                copy.wait_recv()
        for condition, copies in sends(i):
            run(condition, copies, "start")

    def at(*by_depth):
        value = by_depth[3]
        for k in (2, 1, 0):
            value = jnp.where(depth == k, by_depth[k], value)
        return value

    slots = [
        at(-1, 4, 8, 8),
        at(4, 8, 8, 8),
        at(4, 8, 8, 9),
        at(4, 8, 8, 9),
        at(8, 9, 10, 10),
        at(8, 9, 10, 10),
        at(8, 9, 10, 11),
        at(10, 11, 11, 11),
    ]

    pl.semaphore_wait(barrier, 8)

    @pl.when(depth == 0)
    def _():
        for copy in own_copies:
            copy.wait()
        event(0)

    for copy in small:
        copy.wait()
    scalar, compact = own_rows(
        v_single[...], v_meta[...], v_wq[...], v_wk[...], v_wqp[...], head_weight, chain_bias
    )
    pack_rows[y, :, :384] = scalar
    pack_rows[y, :, 384:] = compact
    key_points, values, value_points = own_weights(v_wkp[...], v_wv[...], v_wvp[...])
    pack_weights[y, :48] = key_points
    pack_weights[y, 48:96] = values
    pack_weights[y, 96:] = value_points

    def exchange(src, dst, sent, received):
        out, arriving = [], []
        for step in (1, 2, 3):
            peer = lax.rem(y + step, 4)
            origin = lax.rem(y + 4 - step, 4)
            out.append(remote(src(peer), dst.at[y], sent + step - 1, received + step - 1, {"head": peer}))
            arriving.append(
                remote(dst.at[origin], dst.at[origin], sent + step - 1, received + step - 1, {"head": peer})
            )
        return out, arriving

    rows_sent, rows_arriving = exchange(lambda peer: pack_rows.at[y], pack_rows, ROWS_OUT, ROWS_IN)
    weights_sent, weights_arriving = exchange(
        lambda peer: pack_weights.at[y], pack_weights, WEIGHTS_OUT, WEIGHTS_IN
    )
    for copy in rows_sent + weights_sent:
        copy.start()

    row, col = iota((32, 128), 0), iota((32, 12), 1)
    pick_row = iota((32, 12), 0)
    first = nt(ones_where(pick_row == col), v_wbias[...])
    second = nt(ones_where(pick_row == col + 12), v_wbias[...])
    bias_rows[:, :128] = first.astype(BF16)
    bias_rows[:, 128:] = second.astype(BF16)

    def bias_step(t, _):
        pltpu.make_async_copy(pair.at[pl.ds(2 * t, 2)], pairs.at[pl.ds(2 * t, 2)], pair_sem.at[t]).wait()
        for c in range(0, CHUNKS, 2):
            block_a = pairs[2 * t, c : c + 2].reshape(2 * KEYS, 128)
            block_b = pairs[2 * t + 1, c : c + 2].reshape(2 * KEYS, 128)
            out = nt(bias_rows[...], jnp.concatenate([block_a, block_b], axis=1))[:GROUP]
            out = short(out) * WEIGHT_L
            bias[c, t] = out[:, :KEYS]
            bias[c + 1, t] = out[:, KEYS:]
        for i in range(6):
            pl.when(slots[i] == t)(lambda i=i: event(i))
        return 0

    lax.fori_loop(0, GROUPS, bias_step, 0)

    for copy in rows_arriving + weights_arriving:
        copy.wait_recv()
    for_single, for_other, factor = all_rows(pack_rows[...].reshape(ROWS, 512))
    rows_single[...] = for_single
    rows_other[...] = for_other
    factors[...] = -factor
    packs = pack_weights[...]
    row, col = iota((ROWS, ROWS), 0), iota((ROWS, ROWS), 1)
    place = row & 15
    pick = col == (place >> 2) * 48 + (row >> 6) * 16 + ((row >> 4) & 3) * 4 + (place & 3)
    w_points[...] = mm(ones_where(pick), packs[:, :48].reshape(ROWS, 384)).astype(BF16)
    w_values[...] = packs[:, 48:96].reshape(ROWS, 384)
    row, col = iota((288, 320), 0), iota((288, 320), 1)
    b = by96(row)
    rest = row - b * 96
    owner = by24(rest)
    pick = col == owner * 80 + b * 24 + rest - owner * 24
    w_vpoints[...] = mm(ones_where(pick), packs[:, 96:].reshape(320, 384)).astype(BF16)

    acc_pair[...] = jnp.zeros_like(acc_pair)
    acc_single[...] = jnp.zeros_like(acc_single)
    acc_points[...] = jnp.zeros_like(acc_points)
    top[...] = jnp.full_like(top, -1e30)
    total[...] = jnp.zeros_like(total)

    indices = [item(i)[2] for i in range(8)]

    def index_of(i):
        value = indices[7]
        for k in range(7):
            value = jnp.where(i == k, indices[k], value)
        return value

    def key_meta(index):
        half = iota((16, 128), 1) < 64
        first, second = metas[index, 0], metas[index, 1]
        start = pltpu.roll(second[:, :128], 64, 1)
        end = pltpu.roll(second[:, 128:], 64, 1)
        return [first[:, :128], jnp.where(half, first[:, 128:], start), jnp.where(half, start, end)]

    def key_step(s, _):
        for i in range(8):
            pl.when(slots[i] == s + 8)(lambda i=i: event(i))
        pair_of = []
        for k in range(2):
            i = 2 * s + k
            index = index_of(i)
            pair_of.append(index)
            here = keys.at[index, 1 - core]
            remote(here, here, 0, CORE_IN + i, {"blk": sibling}).wait_recv()
            here = metas.at[index, 1 - core]
            remote(here, here, 0, META + CORE_IN + i, {"blk": sibling}).wait_recv()

        single = jnp.concatenate([keys[index].reshape(KEYS, 384) for index in pair_of], axis=0)
        meta = jnp.concatenate(key_meta(pair_of[0]) + key_meta(pair_of[1]), axis=1)

        def placed(local, rows):
            result = []
            for a in range(3):
                moved = meta[9 + a : 10 + a] + meta[3 * a : 3 * a + 1] * local[:rows]
                moved = moved + meta[3 * a + 1 : 3 * a + 2] * local[rows : 2 * rows]
                moved = moved + meta[3 * a + 2 : 3 * a + 3] * local[2 * rows :]
                result.append(moved.astype(BF16))
            return result

        points = placed(nt(w_points[...], single), 64)
        square = 0.0
        for part in points:
            wide = part.astype(F32)
            square = square + wide * wide
        norm = square[:16] + square[16:32] + square[32:48] + square[48:]
        norms = [v.astype(BF16) for v in split3(norm * factors[...])]
        width = 2 * KEYS
        chains = ones_where(meta[12:13] == iota((32, width), 0).astype(F32))
        others = jnp.concatenate(
            points + points + [chains, chains] + norms + [jnp.full((16, width), 1.0, BF16)], axis=0
        )
        logit = nt(rows_single[...], single) + mm(rows_other[...], others)
        logit = logit + jnp.concatenate([bias[index].reshape(ROWS, KEYS) for index in pair_of], axis=1)
        logit = jnp.where(meta[13:14] > 0.5, logit, -1000000000.0)
        old = top[...]
        new = jnp.maximum(old, jnp.max(logit, axis=1, keepdims=True))
        scale = jnp.exp(old - new)
        weight = jnp.exp(logit - new)
        top[...] = new
        total[...] = total[...] * scale + jnp.sum(weight, axis=1, keepdims=True)
        weight_b = weight.astype(BF16)
        acc_single[...] = acc_single[...] * scale + mm(weight_b, single)
        vpoints = jnp.concatenate(placed(nt(w_vpoints[...], single), 96), axis=0)
        acc_points[...] = acc_points[...] * scale + nt(weight_b, vpoints)
        upper_rows = iota((GROUP, 128), 0) < 12
        for g in range(GROUPS):
            lo = g * GROUP
            there = jnp.concatenate(
                [
                    jnp.concatenate([pairs[2 * g, index] for index in pair_of], axis=0),
                    jnp.concatenate([pairs[2 * g + 1, index] for index in pair_of], axis=0),
                ],
                axis=1,
            )
            out = mm(weight[lo : lo + GROUP].astype(BF16), there)
            out = jnp.where(upper_rows, out[:, :128], out[:, 128:])
            acc_pair[g] = acc_pair[g] * scale[lo : lo + GROUP] + out
        return 0

    lax.fori_loop(0, 4, key_step, 0)

    inverse = 1.0 / total[...]
    row = iota((ROWS, 1), 0)
    head = row - by12(row) * 12
    pair_part = (acc_pair[...].reshape(ROWS, 128) * inverse).astype(BF16)
    hi, lo = split2(acc_single[...] * inverse)
    scalar = nt(hi.astype(BF16), w_values[...]) + nt(lo.astype(BF16), w_values[...])
    scalar = jnp.where((iota((ROWS, ROWS), 1) >> 4) == head, scalar, 0.0).astype(BF16)
    fold = ones_where((iota((ROWS, 128), 0) & 15) == iota((ROWS, 128), 1))
    other = mm(scalar, fold)
    col = iota((1, 288), 1)
    rest = col - by96(col) * 96
    hi, lo = split2(jnp.where((rest >> 3) == head, acc_points[...] * inverse, 0.0))
    source, lane = iota((288, 128), 0), iota((288, 128), 1)
    b = by96(source)
    target = b * 8 + (source & 7)
    other = other + mm(hi.astype(BF16), ones_where(lane == target + 16))
    other = other + mm(lo.astype(BF16), ones_where(lane == target + 40))
    lane = iota((1, 128), 1)
    for start, value in ((64, top[...]), (67, total[...])):
        for step, piece in enumerate(split3(value)):
            other = jnp.where(lane == start + step, piece, other)
    row, col = iota((ROWS, ROWS), 0), iota((ROWS, ROWS), 1)
    query = by12(col)
    pick = ones_where(((row & 15) == query) & ((row >> 4) == col - query * 12))
    moved = mm(pick, jnp.concatenate([pair_part, other.astype(BF16)], axis=1)).astype(BF16)
    part_out[...] = moved.reshape(4, 48, 256)

    parts_sent, parts_arriving = exchange(lambda peer: part_out.at[peer], part_in, PART_OUT, PART_IN)
    for copy in parts_sent:
        copy.start()
    part_in[y] = part_out[y]
    for copy in parts_arriving:
        copy.wait_recv()

    parts = [part_in[k].astype(F32) for k in range(4)]
    tops = [p[:, 192:193] + p[:, 193:194] + p[:, 194:195] for p in parts]
    best = jnp.maximum(jnp.maximum(tops[0], tops[1]), jnp.maximum(tops[2], tops[3]))
    shares = [
        (p[:, 195:196] + p[:, 196:197] + p[:, 197:198]) * jnp.exp(t - best) for p, t in zip(parts, tops)
    ]
    inverse = 1.0 / (shares[0] + shares[1] + shares[2] + shares[3])
    sums = sum(p * (s * inverse) for p, s in zip(parts, shares))
    o_pair = sums[:, :128].astype(BF16)
    other = sums[:, 128:]
    frames = nt(ones_where((iota((48, 16), 0) & 15) == iota((48, 16), 1), F32), v_meta[...], HIGH)
    lane = iota((1, 128), 1)
    inside = (lane >= 16) & (lane < 40)
    axis = (lane - 16) >> 3
    point = lane & 7
    source = iota((128, 128), 0)
    entry = iota((16, 128), 0)
    located = 0.0
    for b in range(3):
        pick = ((source == point + 16 + 8 * b) | (source == point + 40 + 8 * b)) & inside
        shifted = mm(other, ones_where(pick, F32), HIGH) - frames[:, 9 + b : 10 + b]
        turn = mm(frames, ones_where((entry == 3 * b + axis) & inside, F32), HIGH)
        located = located + turn * shifted
    square = located * located
    last = (lane >= 40) & (lane < 48)
    pick = (source >= 16) & (source < 40) & ((source & 7) == point) & last
    length = jnp.sqrt(mm(square, ones_where(pick, F32), HIGH) + 1e-08)
    feats = jnp.where(lane < 16, other, jnp.where(inside, located, jnp.where(last, length, 0.0)))
    feats = feats.astype(BF16)[:, :48]
    update = 0.0
    for k in range(3):
        here = slice(16 * k, 16 * k + 16)
        w = 176 * k
        update = update + mm(o_pair[here], v_wout[w + 16 : w + 144])
        rest = jnp.concatenate([v_wout[w : w + 16], v_wout[w + 144 : w + 176]], axis=0)
        update = update + mm(feats[here], rest)
    updates[y] = update
    updates_sent, updates_arriving = exchange(lambda peer: updates.at[y], updates, UPDATE_OUT, UPDATE_IN)
    for copy in updates_sent:
        copy.start()
    for copy in updates_arriving:
        copy.wait_recv()

    mixed = v_single[...].astype(F32) + updates[0] + updates[1] + updates[2] + updates[3]
    mean = jnp.mean(mixed, axis=1, keepdims=True)
    centered = mixed - mean
    var = jnp.mean(centered * centered, axis=1, keepdims=True)
    out = (centered / jnp.sqrt(var + 1e-05) * v_gain[...]).astype(BF16)
    single_out[...] = out
    w_rows = nt(ones_where(iota((16, 6), 0) == iota((16, 6), 1)), v_wframe[...]).astype(BF16)
    shift = nt(w_rows, out)
    u = [shift[k : k + 1] for k in range(6)]
    length = jnp.sqrt(1.0 + u[0] * u[0] + u[1] * u[1] + u[2] * u[2])
    turn = quat_rotation(1.0 / length, u[0] / length, u[1] / length, u[2] / length)
    rot = [v_meta[k : k + 1] for k in range(12)]
    for a in range(3):
        for c in range(3):
            k = 3 * a + c
            frames_out[k : k + 1] = (
                rot[3 * a] * turn[c] + rot[3 * a + 1] * turn[3 + c] + rot[3 * a + 2] * turn[6 + c]
            )
        moved = rot[3 * a] * u[3] + rot[3 * a + 1] * u[4] + rot[3 * a + 2] * u[5]
        frames_out[9 + a : 10 + a] = moved + rot[9 + a]

    for i in range(8):
        for condition, copies in sends(i):
            run(condition, copies, "wait_send")
    for copy in rows_sent + weights_sent + parts_sent + updates_sent:
        copy.wait_send()


def per_device(
    query_single, query_frames, query_chain, key_single, key_frames, key_chain, key_mask, pair,
    w_q, w_k, w_v, w_qp, w_kp, w_vp, w_bias, head_weight, chain_bias, w_out, ln_gain, w_frame,
):
    chain_q = query_chain.astype(F32)[None]
    meta_q = jnp.concatenate([query_frames, chain_q, jnp.zeros((3, 16), F32)], axis=0)
    codes = jnp.stack([key_chain, key_mask]).astype(F32)
    meta_k = jnp.concatenate([key_frames, codes, jnp.zeros((2, 192), F32)], axis=0)
    meta_k = jnp.pad(meta_k, ((0, 0), (0, 64)))
    pair = pair.reshape(16, CHUNKS, KEYS, 128)
    vm = pltpu.VMEM
    anywhere = pl.BlockSpec(memory_space=pl.ANY)
    scalars = pl.BlockSpec(memory_space=pltpu.SMEM)
    inside = pl.BlockSpec(memory_space=pltpu.VMEM)
    return pl.pallas_call(
        kernel,
        out_shape=(jax.ShapeDtypeStruct((16, 384), BF16), jax.ShapeDtypeStruct((12, 16), F32)),
        in_specs=[anywhere] * 15 + [scalars] * 2,
        out_specs=(inside, inside),
        scratch_shapes=[
            vm((16, 384), BF16), vm((16, 16), F32), vm((384, 48), BF16), vm((384, 48), BF16),
            vm((384, 48), BF16), vm((384, 36), BF16), vm((384, 36), BF16), vm((384, 72), BF16),
            vm((128, 12), BF16), vm((528, 384), BF16), vm((1, 384), F32), vm((384, 6), BF16),
            vm((16, CHUNKS, KEYS, 128), BF16), vm((CHUNKS, 2, 192, 384), BF16), vm((CHUNKS, 2, 16, 256), F32),
            vm((CHUNKS, GROUPS, GROUP, KEYS), F32), vm((4, 48, 512), BF16), vm((4, 176, 384), BF16),
            vm((ROWS, 384), BF16), vm((ROWS, 512), BF16), vm((ROWS, 384), BF16), vm((ROWS, 384), BF16),
            vm((288, 384), BF16), vm((16, 1), F32), vm((32, 256), BF16),
            vm((GROUPS, GROUP, 128), F32), vm((ROWS, 384), F32), vm((ROWS, 288), F32),
            vm((ROWS, 1), F32), vm((ROWS, 1), F32),
            vm((4, 48, 256), BF16), vm((4, 48, 256), BF16), vm((4, 16, 384), F32),
            pltpu.SemaphoreType.DMA((14,)), pltpu.SemaphoreType.DMA((GROUPS,)),
            pltpu.SemaphoreType.DMA((64,)), pltpu.SemaphoreType.DMA((64,)),
        ],
        compiler_params=pltpu.CompilerParams(
            collective_id=0, has_side_effects=True, vmem_limit_bytes=56 * 1024 * 1024
        ),
    )(
        query_single, meta_q, key_single, meta_k, pair, w_q, w_k, w_v, w_qp, w_kp, w_vp, w_bias, w_out,
        ln_gain[None], w_frame, head_weight, chain_bias,
    )


def solution(mesh):
    rows = ("sample", "blk")
    heads = P(None, "head")
    in_specs = (
        P(rows, None), P(None, rows), P(rows), P(rows, None), P(None, rows), P(rows), P(rows),
        P(rows, "head", None), heads, heads, heads, heads, heads, heads, P(), P("head"), P("head"),
        P(), P(), P(),
    )
    out_specs = (P(rows, None), P(None, rows))
    return jax.shard_map(
        per_device, mesh=mesh, in_specs=in_specs, out_specs=out_specs, check_vma=False
    )
```

profile of v0, /device:TPU:22, one launch (start us, length us, event | category | flops | bytes accessed | tf_op | source)
XLA Modules:
  0.0 82.1 jit_solution(1716276594014903771)
XLA Ops:
  0.6 0.7 convert_bitcast_fusion
  1.3 0.1 pad.7.clone
  1.4 0.1 pad.12.clone
  1.4 1.2 %broadcast_in_dim.15.gain = f32[1,384]{1,0:T(1,128)} reshape(f32[384]{0:T(512)} %param.38) | data formatting | bytes 3072 | tf_op jit(solution)/shard_map/broadcast_in_dim | solution.py:667
  2.7 0.7 add_convert_fusion
  3.4 1.4 %maximum_maximum_fusion.1.meta_q = f32[16,16]{1,0:T(8,128)} fusion(f32[1,16]{1,0:T(1,128)S(1)} %convert_bitcast_fusion, f32[12,16]{1,0:T(8,128)} %param.21, f32[16]{0:T(128)S(1)} %pad.12.clone), kind=kLoop, calls=%fused_computation.1 | loop fusion | flops 512 | bytes 1920 | tf_op jit(solution)/shard_map/concatenate | solution.py:634
  4.8 0.8 maximum_maximum_fusion
  5.6 0.6 pad.4.meta_k
  6.2 1.4 %copy.28.w_bias = bf16[128,12]{1,0:T(8,128)(2,1)} copy(bf16[128,12]{0,1:T(8,128)(2,1)} %param.34) | data formatting | bytes 6144 | tf_op args[14]
  7.6 1.5 %copy.22.w_q = bf16[384,48]{1,0:T(8,128)(2,1)} copy(bf16[384,48]{0,1:T(8,128)(2,1)} %param.28) | data formatting | bytes 73728 | tf_op args[8]
  9.1 1.5 %copy.23.w_k = bf16[384,48]{1,0:T(8,128)(2,1)} copy(bf16[384,48]{0,1:T(8,128)(2,1)} %param.29) | data formatting | bytes 73728 | tf_op args[9]
  10.6 1.5 %copy.24.w_v = bf16[384,48]{1,0:T(8,128)(2,1)} copy(bf16[384,48]{0,1:T(8,128)(2,1)} %param.30) | data formatting | bytes 73728 | tf_op args[10]
  12.1 1.5 %copy.25.w_qp = bf16[384,36]{1,0:T(8,128)(2,1)} copy(bf16[384,36]{0,1:T(8,128)(2,1)} %param.31) | data formatting | bytes 55296 | tf_op args[11]
  13.6 1.5 %copy.26.w_kp = bf16[384,36]{1,0:T(8,128)(2,1)} copy(bf16[384,36]{0,1:T(8,128)(2,1)} %param.32) | data formatting | bytes 55296 | tf_op args[12]
  15.1 1.6 %copy.27.w_vp = bf16[384,72]{1,0:T(8,128)(2,1)} copy(bf16[384,72]{0,1:T(8,128)(2,1)} %param.33) | data formatting | bytes 110592 | tf_op args[13]
  16.7 1.5 %copy.29.w_frame = bf16[384,6]{1,0:T(8,128)(2,1)} copy(bf16[384,6]{0,1:T(8,128)(2,1)} %param.39) | data formatting | bytes 9216 | tf_op args[19]
  18.1 61.4 %shard_map.203 = (bf16[16,384]{1,0:T(8,128)(2,1)}, f32[12,16]{1,0:T(8,128)}) custom-call(bf16[16,384]{1,0:T(8,128)(2,1)} %single_q.1, f32[16,16]{1,0:T(8,128)} %maximum_maximum_fusion.1.meta_q, bf16[192,384]{1,0:T(8,128)(2,1)} %single_k.1, f32[16,256]{1,0:T(8,128)} %pad.4.meta_k, bf16[16,8,384,128]{3,2,1,0:T(8,128)(2,1)} %bitcast.5, ...), custom_call_target="tpu_custom_call" | custom-call | tf_op jit(solution)/shard_map/pallas_call | solution.py:643
  79.5 1.3 %copy.32 = bf16[16,384]{1,0:T(8,128)(2,1)} copy(bf16[16,384]{1,0:T(8,128)(2,1)} %get-tuple-element.4) | data formatting | bytes 24576
  80.8 1.3 %copy.33 = f32[12,16]{1,0:T(8,128)} copy(f32[12,16]{1,0:T(8,128)} %get-tuple-element.5) | data formatting | bytes 1536
  (2 shorter events, 0.0 us)
where the time goes:
time: 82.9 us; the launch traced here: 82.1 us
  Pallas kernels  61.4 us (74%)
  local copies, waits for them, and re-layouts  16.6 us (20%)
  other arithmetic  3.52 us (4%)
    pallas_call x1, Pallas kernels, per_device(): pl.pallas_call(kernel, out_shape=(jax.ShapeDtypeStruct((16, 384), BF16),...  61.4 us
    unnamed x10, local copies, waits for them, and re-layouts  14.6 us

commit v1 on v0

--- a/solution.py
+++ b/solution.py
@@ -17,15 +17,25 @@
 ROWS = 192
 GROUPS = 8
 GROUP = 24
+EVENTS = {
+    "z0": (0, 0, 0), "z1": (0, 1, 0), "l0": (1, 0, 0), "r0": (2, 0, 0), "z2": (0, 0, 1), "l1": (1, 1, 0),
+    "r1": (2, 1, 0), "z3": (0, 1, 1), "l2": (1, 0, 1), "r2": (2, 0, 1), "l3": (1, 1, 1), "r3": (2, 1, 1),
+    "o0": (3, 0, 1), "o1": (3, 1, 1),
+}
+SLOTS = {
+    "z0": (-1, 4, 8), "z1": (4, 6, 8), "l0": (4, 8, 8), "r0": (4, 8, 8), "z2": (-1, 8, 8), "l1": (7, 8, 8),
+    "r1": (7, 8, 8), "z3": (6, 8, 8), "l2": (5, 9, 9), "r2": (5, 9, 9), "l3": (8, 9, 9), "r3": (8, 9, 9),
+    "o0": (10, 10, 10), "o1": (11, 11, 11),
+}
 CHUNKS = 8
 KEYS = 384
 WEIGHT_L = math.sqrt(1.0 / 3.0)
 WEIGHT_C = math.sqrt(2.0 / (9.0 * QPTS))
 
-Z_IN, LEFT_IN, RIGHT_IN, HALF_LEFT_IN, HALF_RIGHT_IN, CORE_IN = 0, 2, 4, 6, 8, 10
-ROWS_IN, WEIGHTS_IN, PART_IN, UPDATE_IN, META = 18, 21, 24, 27, 30
-Z_OUT, Z_BACK, RIGHT_OUT, LEFT_OUT, HALF_RIGHT_OUT, HALF_LEFT_OUT, CORE_OUT = 0, 2, 3, 5, 7, 9, 11
-ROWS_OUT, WEIGHTS_OUT, PART_OUT, UPDATE_OUT, META_OUT = 19, 22, 25, 28, 31
+Z_IN, LEFT_IN, RIGHT_IN, HALF_LEFT_IN, HALF_RIGHT_IN, CORE_IN = 0, 4, 8, 12, 14, 16
+ROWS_IN, WEIGHTS_IN, PART_IN, META = 24, 27, 30, 33
+Z_OUT, Z_BACK, Z_LAST, RIGHT_OUT, LEFT_OUT, HALF_RIGHT_OUT, HALF_LEFT_OUT, CORE_OUT = 0, 4, 8, 12, 16, 20, 22, 24
+ROWS_OUT, WEIGHTS_OUT, PART_OUT, META_OUT = 32, 35, 38, 41
 
 
 def iota(shape, dim):
@@ -106,20 +116,21 @@
     ]
 
 
-def own_rows(single, meta, w_q, w_k, w_qp, head_weight, chain_bias):
+def own_rows(single, frames, chain, w_q, w_k, w_qp, head_weight, chain_bias):
     rows = 48
     row = iota((rows, 1), 0)
     query = by3(row)
     local_head = row - query * 3
     spread = query == iota((rows, 16), 1)
     single_rows = mm(ones_where(spread), single).astype(BF16)
-    q_s = mm(single_rows, w_q).astype(BF16).astype(F32)
+    q_s = nt(single_rows, w_q).astype(BF16).astype(F32)
     col = iota((rows, 48), 1)
     q_s = jnp.where((col >> 4) == local_head, q_s, 0.0).astype(BF16)
-    scalar = nt(q_s, w_k) * (WEIGHT_L / 4.0)
-
-    frames = nt(ones_where(spread, F32), meta, HIGH)
-    local = mm(single_rows, w_qp)
+    scalar = mm(q_s, w_k) * (WEIGHT_L / 4.0)
+
+    frames = nt(ones_where(spread, F32), frames, HIGH)
+    own_chain = jnp.sum(jnp.where(spread, chain.astype(F32), 0.0), axis=1, keepdims=True)
+    local = nt(single_rows, w_qp)
     col = iota((rows, 36), 1)
     local = jnp.where(by12(col) == local_head, local, 0.0)
     lane = iota((1, 128), 1)
@@ -129,7 +140,7 @@
     inside = lane < 24
     source = iota((36, 128), 0)
     source = source - by12(source) * 12
-    entry = iota((16, 128), 0)
+    entry = iota((12, 128), 0)
     placed = mm(frames, ones_where((entry == axis + 9) & inside, F32), HIGH)
     for b in range(3):
         here = mm(local, ones_where((source == point + 4 * b) & inside, F32), HIGH)
@@ -145,7 +156,6 @@
     coeff = soft * (WEIGHT_L * WEIGHT_C / 2.0)
     point_hi, point_lo = split2(2.0 * coeff * placed)
     chain_hi, chain_lo = split2(per_head(chain_bias) * WEIGHT_L)
-    own_chain = frames[:, 12:13]
     lane_f = lane.astype(F32)
     compact = jnp.where(lane < 12, point_hi, jnp.where(inside, point_lo, 0.0))
     compact = jnp.where((lane >= 24) & (lane < 48) & (own_chain == lane_f - 24.0), chain_hi, compact)
@@ -161,15 +171,14 @@
     col = iota((48, 36), 1)
     head = row & 3
     pick = (col == head * 12 + (row >> 4) * 4 + ((row >> 2) & 3)) & (head < 3)
-    key_points = nt(ones_where(pick), w_kp).astype(BF16)
-    values = nt(ones_where(iota((48, 48), 0) == iota((48, 48), 1)), w_v).astype(BF16)
+    key_points = mm(ones_where(pick), w_kp).astype(BF16)
     row = iota((80, 72), 0)
     col = iota((80, 72), 1)
     b = by24(row)
     rest = row - b * 24
     pick = (col == (rest >> 3) * 24 + b * 8 + (rest & 7)) & (row < 72)
-    value_points = nt(ones_where(pick), w_vp).astype(BF16)
-    return key_points, values, value_points
+    value_points = mm(ones_where(pick), w_vp).astype(BF16)
+    return key_points, w_v, value_points
 
 
 def all_rows(packs):
@@ -203,14 +212,13 @@
 
 
 def kernel(
-    single_q, meta_q, single_k, meta_k, pair, w_q, w_k, w_v, w_qp, w_kp, w_vp, w_bias, w_out, gain, w_frame,
-    head_weight, chain_bias,
-    single_out, frames_out,
-    v_single, v_meta, v_wq, v_wk, v_wv, v_wqp, v_wkp, v_wvp, v_wbias, v_wout, v_gain, v_wframe,
+    single_q, frames_q, chain_q, single_k, frames_k, chain_k, mask_k, pair, w_q, w_k, w_v, w_qp, w_kp, w_vp, w_bias,
+    w_out, head_weight, chain_bias,
+    mixed_out,
+    v_single, v_frames, v_chain, v_kframes, v_kchain, v_kmask, v_wq, v_wk, v_wv, v_wqp, v_wkp, v_wvp, v_wbias, v_wout,
     pairs, keys, metas, bias, pack_rows, pack_weights,
     rows_single, rows_other, w_points, w_values, w_vpoints, factors, bias_rows,
-    acc_pair, acc_single, acc_points, top, total,
-    part_out, part_in, updates,
+    acc_pair, acc_single, acc_points, top, total, part_in,
     local_sem, pair_sem, send_sem, recv_sem,
 ):
     y = lax.axis_index("head")
@@ -220,46 +228,58 @@
     x = lax.rem(lax.div(blk, 2), 4)
     r = lax.rem(z - 2 * y + 8, 8)
     upper = (r >= 1) & (r <= 4)
-    depth = jnp.where(upper, r - 1, lax.rem(8 - r, 8))
-    step_z = jnp.where(upper, 1, -1)
+    depth = jnp.where(r <= 1, 0, jnp.where((r == 3) | (r == 6), 1, 2))
     near = jnp.where(upper, 1, 0)
 
     def device(zz, xx, cc):
         return (zz * 4 + xx) * 2 + cc
 
-    out_z = device(lax.rem(z + step_z + 8, 8), x, core)
-    in_z = device(lax.rem(z - step_z + 8, 8), x, core)
+    partner = device(lax.rem(z + jnp.where(r == 0, 1, 7), 8), x, core)
+    above, below = device(lax.rem(z + 1, 8), x, core), device(lax.rem(z + 7, 8), x, core)
+    first_relay = device(lax.rem(2 * y + 3, 8), x, core)
+    second_relay = device(lax.rem(2 * y + 6, 8), x, core)
     right = device(z, lax.rem(x + 1, 4), core)
     left = device(z, lax.rem(x + 3, 4), core)
     sibling = device(z, x, 1 - core)
 
     small = [
-        (single_q, v_single), (meta_q, v_meta), (w_q, v_wq), (w_k, v_wk), (w_qp, v_wqp), (w_kp, v_wkp),
-        (w_v, v_wv), (w_vp, v_wvp), (w_bias, v_wbias), (gain, v_gain), (w_frame, v_wframe),
-        (w_out.at[pl.ds(pl.multiple_of(y * 528, 528), 528)], v_wout),
+        (single_q, v_single), (frames_q, v_frames), (chain_q, v_chain), (w_q, v_wq), (w_k, v_wk), (w_qp, v_wqp),
+        (w_kp, v_wkp), (w_v, v_wv), (w_vp, v_wvp), (w_bias, v_wbias),
     ]
     small = [pltpu.make_async_copy(src, dst, local_sem.at[i]) for i, (src, dst) in enumerate(small)]
 
-    def item(i):
-        phase = 0 if i in (0, 1, 2, 6) else 1
-        kind = i if i < 3 else (i - 3 if i < 6 else 3)
+    def item(phase, kind):
         plane = near if phase == 0 else 1 - near
-        return phase, kind, plane * 4 + lax.rem(x + (0, 3, 1, 2)[kind], 4)
-
-    own_index = item(0)[2]
+        return plane * 4 + lax.rem(x + (0, 3, 1, 2)[kind], 4)
+
+    def chunk_of(phase, kind):
+        return (phase, 2 + 2 * phase, 3 + 2 * phase, 6 + phase)[kind]
+
+    own_index = item(0, 0)
     own_copies = [
-        pltpu.make_async_copy(single_k, keys.at[own_index, core], local_sem.at[12]),
-        pltpu.make_async_copy(meta_k, metas.at[own_index, core], local_sem.at[13]),
+        pltpu.make_async_copy(src, dst, local_sem.at[10 + i])
+        for i, (src, dst) in enumerate(
+            ((single_k, keys.at[own_index, core]), (frames_k, v_kframes), (chain_k, v_kchain), (mask_k, v_kmask))
+        )
     ]
+    out_copy = pltpu.make_async_copy(w_out, v_wout, local_sem.at[14])
     pair_copies = [
         pltpu.make_async_copy(pair.at[pl.ds(2 * g, 2)], pairs.at[pl.ds(2 * g, 2)], pair_sem.at[g])
         for g in range(GROUPS)
     ]
 
     barrier = pltpu.get_barrier_semaphore()
-    for other in (
-        device(lax.rem(z + 1, 8), x, core), device(lax.rem(z + 7, 8), x, core), right, left, sibling
-    ):
+    along_z = [(depth == 0, partner), (depth == 0, first_relay), (depth == 0, second_relay)]
+    along_z += [(depth == 1, above), (depth == 1, below)]
+    along_z += [(depth == 1, device(lax.rem(2 * y, 8), x, core)), (depth == 1, device(lax.rem(2 * y + 1, 8), x, core))]
+    along_z += [(depth == 2, device(lax.rem(2 * y + jnp.where(upper, 3, 6), 8), x, core))]
+    for condition, other in along_z:
+
+        @pl.when(condition)
+        def _(other=other):
+            pl.semaphore_signal(barrier, inc=1, device_id={"blk": other}, device_id_type=MESH)
+
+    for other in (right, left, sibling):
         pl.semaphore_signal(barrier, inc=1, device_id={"blk": other}, device_id_type=MESH)
     for step in (1, 2, 3):
         pl.semaphore_signal(
@@ -275,6 +295,7 @@
         copy.start()
     for copy in pair_copies:
         copy.start()
+    out_copy.start()
 
     def remote(src, dst, sent, received, target):
         return pltpu.make_async_remote_copy(
@@ -282,32 +303,45 @@
             device_id=target, device_id_type=MESH,
         )
 
-    def block(index, cc, sent, received, target, part=None, meta=True):
+    def block(index, cc, sent, received, target, half=None, meta=True):
         ref = keys.at[index, cc]
-        if part is not None:
-            ref = keys.at[index, cc, pl.ds(96 * part, 96)]
+        if half is not None:
+            ref = keys.at[index, cc, pl.ds(96 * half, 96)]
         copies = [remote(ref, ref, sent, received, {"blk": target})]
         if meta:
             ref = metas.at[index, cc]
             copies.append(remote(ref, ref, sent + META_OUT, received + META, {"blk": target}))
         return copies
 
-    def sends(i):
-        phase, kind, index = item(i)
+    def sends(name):
+        kind, phase, half = EVENTS[name]
+        index = item(phase, kind)
         result = []
+        step = 2 * phase + half
+        meta = half == 0
+
+        def add(condition, sent, received, target):
+            result.append((condition, block(index, core, sent, received, target, half, meta)))
+
         if kind == 0:
-            result.append((depth < 3, block(index, core, Z_OUT + phase, Z_IN + phase, out_z)))
             if phase == 0:
-                result.append((depth == 0, block(index, core, Z_BACK, Z_IN + 1, in_z)))
-            result.append((None, block(index, core, RIGHT_OUT + phase, LEFT_IN + phase, right)))
-            result.append((None, block(index, core, LEFT_OUT + phase, RIGHT_IN + phase, left)))
-        if kind == 1:
-            result.append((None, block(index, core, HALF_RIGHT_OUT + phase, HALF_LEFT_IN + phase, right, 0)))
-        if kind == 2:
-            result.append(
-                (None, block(index, core, HALF_LEFT_OUT + phase, HALF_RIGHT_IN + phase, left, 1, False))
-            )
-        result.append((None, block(index, core, CORE_OUT + i, CORE_IN + i, sibling)))
+                far = Z_IN + 2 + half
+                add(depth == 0, Z_OUT + half, far, partner)
+                add(r == 1, Z_BACK + half, Z_IN + half, first_relay)
+                add(r == 1, Z_LAST + half, far, second_relay)
+                add(r == 0, Z_BACK + half, Z_IN + half, second_relay)
+                add(r == 0, Z_LAST + half, far, first_relay)
+            add(depth == 1, Z_OUT + step, Z_IN + step, above)
+            add(depth == 1, Z_BACK + step, Z_IN + step, below)
+            add(None, RIGHT_OUT + step, LEFT_IN + step, right)
+            add(None, LEFT_OUT + step, RIGHT_IN + step, left)
+        if kind == 1 and half == 0:
+            add(None, HALF_RIGHT_OUT + phase, HALF_LEFT_IN + phase, right)
+        if kind == 2 and half == 1:
+            add(None, HALF_LEFT_OUT + phase, HALF_RIGHT_IN + phase, left)
+        if half == 1:
+            i = chunk_of(phase, kind)
+            result.append((None, block(index, core, CORE_OUT + i, CORE_IN + i, sibling)))
         return result
 
     def run(condition, copies, verb):
@@ -320,52 +354,44 @@
         else:
             pl.when(condition)(act)
 
-    def event(i):
-        phase, kind, index = item(i)
-        if kind == 0:
-            arriving = block(index, core, 0, Z_IN + phase, sibling)
-            run(depth > 0 if phase == 0 else None, arriving, "wait_recv")
-        elif kind == 3:
-            first = block(index, core, 0, HALF_LEFT_IN + phase, sibling, 0)
-            second = block(index, core, 0, HALF_RIGHT_IN + phase, sibling, 1, False)
-            for copy in first + second:
-                copy.wait_recv()
+    def event(name):
+        kind, phase, half = EVENTS[name]
+        index = item(phase, kind)
+        step = 2 * phase + half
+        if kind == 3:
+            arriving = block(index, core, 0, HALF_LEFT_IN + phase, sibling, 0)
+            arriving += block(index, core, 0, HALF_RIGHT_IN + phase, sibling, 1, False)
         else:
-            place = (LEFT_IN, RIGHT_IN)[kind - 1] + phase
-            for copy in block(index, core, 0, place, sibling):
-                copy.wait_recv()
-        for condition, copies in sends(i):
+            place = (Z_IN, LEFT_IN, RIGHT_IN)[kind] + step
+            arriving = block(index, core, 0, place, sibling, half, half == 0)
+        run(depth > 0 if kind == 0 and phase == 0 else None, arriving, "wait_recv")
+        for condition, copies in sends(name):
             run(condition, copies, "start")
 
-    def at(*by_depth):
-        value = by_depth[3]
-        for k in (2, 1, 0):
-            value = jnp.where(depth == k, by_depth[k], value)
-        return value
-
-    slots = [
-        at(-1, 4, 8, 8),
-        at(4, 8, 8, 8),
-        at(4, 8, 8, 9),
-        at(4, 8, 8, 9),
-        at(8, 9, 10, 10),
-        at(8, 9, 10, 10),
-        at(8, 9, 10, 11),
-        at(10, 11, 11, 11),
-    ]
-
-    pl.semaphore_wait(barrier, 8)
+    slots = {
+        name: jnp.where(depth == 0, when[0], jnp.where(depth == 1, when[1], when[2])) for name, when in SLOTS.items()
+    }
+
+    def events_at(step, names):
+        for name in names:
+            pl.when(slots[name] == step)(lambda name=name: event(name))
 
     @pl.when(depth == 0)
     def _():
         for copy in own_copies:
             copy.wait()
-        event(0)
+        metas[own_index, core] = jnp.zeros((16, 256), F32)
+        metas[own_index, core, :12, :192] = v_kframes[...]
+        metas[own_index, core, 12:13, :192] = v_kchain[...].astype(F32)
+        metas[own_index, core, 13:14, :192] = v_kmask[...].astype(F32)
+
+    pl.semaphore_wait(barrier, jnp.where(depth == 0, 9, jnp.where(depth == 1, 10, 7)))
+    events_at(-1, ["z0", "z2"])
 
     for copy in small:
         copy.wait()
     scalar, compact = own_rows(
-        v_single[...], v_meta[...], v_wq[...], v_wk[...], v_wqp[...], head_weight, chain_bias
+        v_single[...], v_frames[...], v_chain[...], v_wq[...], v_wk[...], v_wqp[...], head_weight, chain_bias
     )
     pack_rows[y, :, :384] = scalar
     pack_rows[y, :, 384:] = compact
@@ -392,10 +418,10 @@
     for copy in rows_sent + weights_sent:
         copy.start()
 
-    row, col = iota((32, 128), 0), iota((32, 12), 1)
+    col = iota((32, 12), 1)
     pick_row = iota((32, 12), 0)
-    first = nt(ones_where(pick_row == col), v_wbias[...])
-    second = nt(ones_where(pick_row == col + 12), v_wbias[...])
+    first = mm(ones_where(pick_row == col), v_wbias[...])
+    second = mm(ones_where(pick_row == col + 12), v_wbias[...])
     bias_rows[:, :128] = first.astype(BF16)
     bias_rows[:, 128:] = second.astype(BF16)
 
@@ -408,11 +434,11 @@
             out = short(out) * WEIGHT_L
             bias[c, t] = out[:, :KEYS]
             bias[c + 1, t] = out[:, KEYS:]
-        for i in range(6):
-            pl.when(slots[i] == t)(lambda i=i: event(i))
+        events_at(t, [name for name, when in SLOTS.items() if any(0 <= k < 8 for k in when)])
         return 0
 
     lax.fori_loop(0, GROUPS, bias_step, 0)
+    events_at(8, [name for name, when in SLOTS.items() if 8 in when])
 
     for copy in rows_arriving + weights_arriving:
         copy.wait_recv()
@@ -439,7 +465,7 @@
     top[...] = jnp.full_like(top, -1e30)
     total[...] = jnp.zeros_like(total)
 
-    indices = [item(i)[2] for i in range(8)]
+    indices = [item(*pair) for pair in ((0, 0), (1, 0), (0, 1), (0, 2), (1, 1), (1, 2), (0, 3), (1, 3))]
 
     def index_of(i):
         value = indices[7]
@@ -455,8 +481,7 @@
         return [first[:, :128], jnp.where(half, first[:, 128:], start), jnp.where(half, start, end)]
 
     def key_step(s, _):
-        for i in range(8):
-            pl.when(slots[i] == s + 8)(lambda i=i: event(i))
+        events_at(jnp.where(s == 0, -2, s + 8), [name for name, when in SLOTS.items() if max(when) > 8])
         pair_of = []
         for k in range(2):
             i = 2 * s + k
@@ -523,93 +548,97 @@
 
     inverse = 1.0 / total[...]
     row = iota((ROWS, 1), 0)
-    head = row - by12(row) * 12
-    pair_part = (acc_pair[...].reshape(ROWS, 128) * inverse).astype(BF16)
+    query = by12(row)
+    head = row - query * 12
+    part_in[y, :ROWS] = (acc_pair[...].reshape(ROWS, 128) * inverse).astype(BF16)
     hi, lo = split2(acc_single[...] * inverse)
     scalar = nt(hi.astype(BF16), w_values[...]) + nt(lo.astype(BF16), w_values[...])
     scalar = jnp.where((iota((ROWS, ROWS), 1) >> 4) == head, scalar, 0.0).astype(BF16)
-    fold = ones_where((iota((ROWS, 128), 0) & 15) == iota((ROWS, 128), 1))
-    other = mm(scalar, fold)
+    lane = iota((1, 128), 1)
+    again = lane & 63
+    source = iota((ROWS, 128), 0)
+    other = mm(scalar, ones_where(((source & 15) == again) & (again < 16)))
+    frames = nt(ones_where(query == iota((ROWS, 16), 1), F32), v_frames[...], HIGH)
     col = iota((1, 288), 1)
-    rest = col - by96(col) * 96
-    hi, lo = split2(jnp.where((rest >> 3) == head, acc_points[...] * inverse, 0.0))
-    source, lane = iota((288, 128), 0), iota((288, 128), 1)
-    b = by96(source)
-    target = b * 8 + (source & 7)
-    other = other + mm(hi.astype(BF16), ones_where(lane == target + 16))
-    other = other + mm(lo.astype(BF16), ones_where(lane == target + 40))
-    lane = iota((1, 128), 1)
-    for start, value in ((64, top[...]), (67, total[...])):
+    axis = by96(col)
+    center = jnp.where(axis == 0, frames[:, 9:10], jnp.where(axis == 1, frames[:, 10:11], frames[:, 11:12]))
+    shifted = jnp.where(((col - axis * 96) >> 3) == head, acc_points[...] * inverse - center, 0.0).astype(BF16)
+    source = iota((288, 128), 0)
+    other = other + mm(shifted, ones_where(again == by96(source) * 8 + (source & 7) + 16))
+    for start, value in ((40, top[...]), (43, total[...])):
         for step, piece in enumerate(split3(value)):
-            other = jnp.where(lane == start + step, piece, other)
-    row, col = iota((ROWS, ROWS), 0), iota((ROWS, ROWS), 1)
-    query = by12(col)
-    pick = ones_where(((row & 15) == query) & ((row >> 4) == col - query * 12))
-    moved = mm(pick, jnp.concatenate([pair_part, other.astype(BF16)], axis=1)).astype(BF16)
-    part_out[...] = moved.reshape(4, 48, 256)
-
-    parts_sent, parts_arriving = exchange(lambda peer: part_out.at[peer], part_in, PART_OUT, PART_IN)
+            other = jnp.where(again == start + step, piece, other)
+    half = ROWS // 2
+    part_in[y, ROWS:] = jnp.where(lane < 64, other[:half], other[half:]).astype(BF16)
+
+    parts_sent, parts_arriving = exchange(lambda peer: part_in.at[y], part_in, PART_OUT, PART_IN)
     for copy in parts_sent:
         copy.start()
-    part_in[y] = part_out[y]
     for copy in parts_arriving:
         copy.wait_recv()
 
-    parts = [part_in[k].astype(F32) for k in range(4)]
-    tops = [p[:, 192:193] + p[:, 193:194] + p[:, 194:195] for p in parts]
+    pair_parts = [part_in[k, :ROWS].astype(F32) for k in range(4)]
+    others = []
+    for k in range(4):
+        both = part_in[k, ROWS:].astype(F32)
+        others.append(jnp.concatenate([both, pltpu.roll(both, 64, 1)], axis=0))
+    tops = [p[:, 40:41] + p[:, 41:42] + p[:, 42:43] for p in others]
     best = jnp.maximum(jnp.maximum(tops[0], tops[1]), jnp.maximum(tops[2], tops[3]))
     shares = [
-        (p[:, 195:196] + p[:, 196:197] + p[:, 197:198]) * jnp.exp(t - best) for p, t in zip(parts, tops)
+        (p[:, 43:44] + p[:, 44:45] + p[:, 45:46]) * jnp.exp(t - best) for p, t in zip(others, tops)
     ]
     inverse = 1.0 / (shares[0] + shares[1] + shares[2] + shares[3])
-    sums = sum(p * (s * inverse) for p, s in zip(parts, shares))
-    o_pair = sums[:, :128].astype(BF16)
-    other = sums[:, 128:]
-    frames = nt(ones_where((iota((48, 16), 0) & 15) == iota((48, 16), 1), F32), v_meta[...], HIGH)
-    lane = iota((1, 128), 1)
+    shares = [share * inverse for share in shares]
+    o_pair = sum(p * s for p, s in zip(pair_parts, shares)).astype(BF16)
+    other = sum(p * s for p, s in zip(others, shares))
     inside = (lane >= 16) & (lane < 40)
     axis = (lane - 16) >> 3
     point = lane & 7
     source = iota((128, 128), 0)
-    entry = iota((16, 128), 0)
+    entry = iota((12, 128), 0)
     located = 0.0
     for b in range(3):
-        pick = ((source == point + 16 + 8 * b) | (source == point + 40 + 8 * b)) & inside
-        shifted = mm(other, ones_where(pick, F32), HIGH) - frames[:, 9 + b : 10 + b]
+        pick = (source == point + 16 + 8 * b) & inside
         turn = mm(frames, ones_where((entry == 3 * b + axis) & inside, F32), HIGH)
-        located = located + turn * shifted
-    square = located * located
+        located = located + turn * mm(other, ones_where(pick, F32), HIGH)
     last = (lane >= 40) & (lane < 48)
     pick = (source >= 16) & (source < 40) & ((source & 7) == point) & last
-    length = jnp.sqrt(mm(square, ones_where(pick, F32), HIGH) + 1e-08)
+    length = jnp.sqrt(mm(located * located, ones_where(pick, F32), HIGH) + 1e-08)
     feats = jnp.where(lane < 16, other, jnp.where(inside, located, jnp.where(last, length, 0.0)))
-    feats = feats.astype(BF16)[:, :48]
-    update = 0.0
-    for k in range(3):
-        here = slice(16 * k, 16 * k + 16)
+    feats = jnp.concatenate([o_pair, feats.astype(BF16)], axis=1)
+    row, col = iota((ROWS, ROWS), 0), iota((ROWS, ROWS), 1)
+    query = by12(col)
+    pick = ones_where(((row & 15) == query) & ((row >> 4) == col - query * 12))
+    feats = mm(pick, feats).astype(BF16)
+    out_copy.wait()
+    update = v_single[...].astype(F32)
+    for k in range(HEADS):
+        here = feats[16 * k : 16 * k + 16]
         w = 176 * k
-        update = update + mm(o_pair[here], v_wout[w + 16 : w + 144])
+        update = update + mm(here[:, :128], v_wout[w + 16 : w + 144])
         rest = jnp.concatenate([v_wout[w : w + 16], v_wout[w + 144 : w + 176]], axis=0)
-        update = update + mm(feats[here], rest)
-    updates[y] = update
-    updates_sent, updates_arriving = exchange(lambda peer: updates.at[y], updates, UPDATE_OUT, UPDATE_IN)
-    for copy in updates_sent:
-        copy.start()
-    for copy in updates_arriving:
-        copy.wait_recv()
-
-    mixed = v_single[...].astype(F32) + updates[0] + updates[1] + updates[2] + updates[3]
+        update = update + mm(here[:, 128:176], rest)
+    mixed_out[...] = update
+
+    for name in EVENTS:
+        for condition, copies in sends(name):
+            run(condition, copies, "wait_send")
+    for copy in rows_sent + weights_sent + parts_sent:
+        copy.wait_send()
+
+
+def finish(mixed_ref, gain, w_frame, frames, single_out, frames_out):
+    mixed = mixed_ref[...]
     mean = jnp.mean(mixed, axis=1, keepdims=True)
     centered = mixed - mean
     var = jnp.mean(centered * centered, axis=1, keepdims=True)
-    out = (centered / jnp.sqrt(var + 1e-05) * v_gain[...]).astype(BF16)
+    out = (centered / jnp.sqrt(var + 1e-05) * gain[...][None]).astype(BF16)
     single_out[...] = out
-    w_rows = nt(ones_where(iota((16, 6), 0) == iota((16, 6), 1)), v_wframe[...]).astype(BF16)
-    shift = nt(w_rows, out)
+    shift = nt(w_frame[...], out)
     u = [shift[k : k + 1] for k in range(6)]
     length = jnp.sqrt(1.0 + u[0] * u[0] + u[1] * u[1] + u[2] * u[2])
     turn = quat_rotation(1.0 / length, u[0] / length, u[1] / length, u[2] / length)
-    rot = [v_meta[k : k + 1] for k in range(12)]
+    rot = [frames[k : k + 1] for k in range(12)]
     for a in range(3):
         for c in range(3):
             k = 3 * a + c
@@ -619,53 +648,48 @@
         moved = rot[3 * a] * u[3] + rot[3 * a + 1] * u[4] + rot[3 * a + 2] * u[5]
         frames_out[9 + a : 10 + a] = moved + rot[9 + a]
 
-    for i in range(8):
-        for condition, copies in sends(i):
-            run(condition, copies, "wait_send")
-    for copy in rows_sent + weights_sent + parts_sent + updates_sent:
-        copy.wait_send()
-
 
 def per_device(
     query_single, query_frames, query_chain, key_single, key_frames, key_chain, key_mask, pair,
     w_q, w_k, w_v, w_qp, w_kp, w_vp, w_bias, head_weight, chain_bias, w_out, ln_gain, w_frame,
 ):
-    chain_q = query_chain.astype(F32)[None]
-    meta_q = jnp.concatenate([query_frames, chain_q, jnp.zeros((3, 16), F32)], axis=0)
-    codes = jnp.stack([key_chain, key_mask]).astype(F32)
-    meta_k = jnp.concatenate([key_frames, codes, jnp.zeros((2, 192), F32)], axis=0)
-    meta_k = jnp.pad(meta_k, ((0, 0), (0, 64)))
     pair = pair.reshape(16, CHUNKS, KEYS, 128)
     vm = pltpu.VMEM
     anywhere = pl.BlockSpec(memory_space=pl.ANY)
     scalars = pl.BlockSpec(memory_space=pltpu.SMEM)
     inside = pl.BlockSpec(memory_space=pltpu.VMEM)
-    return pl.pallas_call(
+    mixed = pl.pallas_call(
         kernel,
-        out_shape=(jax.ShapeDtypeStruct((16, 384), BF16), jax.ShapeDtypeStruct((12, 16), F32)),
-        in_specs=[anywhere] * 15 + [scalars] * 2,
-        out_specs=(inside, inside),
+        out_shape=jax.ShapeDtypeStruct((16, 384), F32),
+        in_specs=[anywhere] * 16 + [scalars] * 2,
+        out_specs=inside,
         scratch_shapes=[
-            vm((16, 384), BF16), vm((16, 16), F32), vm((384, 48), BF16), vm((384, 48), BF16),
-            vm((384, 48), BF16), vm((384, 36), BF16), vm((384, 36), BF16), vm((384, 72), BF16),
-            vm((128, 12), BF16), vm((528, 384), BF16), vm((1, 384), F32), vm((384, 6), BF16),
+            vm((16, 384), BF16), vm((12, 16), F32), vm((1, 16), jnp.int32), vm((12, 192), F32),
+            vm((1, 192), jnp.int32), vm((1, 192), jnp.int32), vm((48, 384), BF16), vm((48, 384), BF16),
+            vm((48, 384), BF16), vm((36, 384), BF16), vm((36, 384), BF16), vm((72, 384), BF16),
+            vm((12, 128), BF16), vm((2112, 384), BF16),
             vm((16, CHUNKS, KEYS, 128), BF16), vm((CHUNKS, 2, 192, 384), BF16), vm((CHUNKS, 2, 16, 256), F32),
             vm((CHUNKS, GROUPS, GROUP, KEYS), F32), vm((4, 48, 512), BF16), vm((4, 176, 384), BF16),
             vm((ROWS, 384), BF16), vm((ROWS, 512), BF16), vm((ROWS, 384), BF16), vm((ROWS, 384), BF16),
             vm((288, 384), BF16), vm((16, 1), F32), vm((32, 256), BF16),
             vm((GROUPS, GROUP, 128), F32), vm((ROWS, 384), F32), vm((ROWS, 288), F32),
-            vm((ROWS, 1), F32), vm((ROWS, 1), F32),
-            vm((4, 48, 256), BF16), vm((4, 48, 256), BF16), vm((4, 16, 384), F32),
-            pltpu.SemaphoreType.DMA((14,)), pltpu.SemaphoreType.DMA((GROUPS,)),
-            pltpu.SemaphoreType.DMA((64,)), pltpu.SemaphoreType.DMA((64,)),
+            vm((ROWS, 1), F32), vm((ROWS, 1), F32), vm((4, 288, 128), BF16),
+            pltpu.SemaphoreType.DMA((15,)), pltpu.SemaphoreType.DMA((GROUPS,)),
+            pltpu.SemaphoreType.DMA((80,)), pltpu.SemaphoreType.DMA((64,)),
         ],
         compiler_params=pltpu.CompilerParams(
             collective_id=0, has_side_effects=True, vmem_limit_bytes=56 * 1024 * 1024
         ),
     )(
-        query_single, meta_q, key_single, meta_k, pair, w_q, w_k, w_v, w_qp, w_kp, w_vp, w_bias, w_out,
-        ln_gain[None], w_frame, head_weight, chain_bias,
+        query_single, query_frames, query_chain[None], key_single, key_frames, key_chain[None], key_mask[None], pair,
+        w_q.T, w_k.T, w_v.T, w_qp.T, w_kp.T, w_vp.T, w_bias.T, w_out, head_weight, chain_bias,
     )
+    return pl.pallas_call(
+        finish,
+        out_shape=(jax.ShapeDtypeStruct((16, 384), BF16), jax.ShapeDtypeStruct((12, 16), F32)),
+        in_specs=[inside] * 4,
+        out_specs=(inside, inside),
+    )(mixed, ln_gain, w_frame.T, query_frames)
 
 
 def solution(mesh):

time: 82.9 us -> 57.3 us (0.69)
  the two profiles are of different devices: /device:TPU:22 before, /device:TPU:1 now
where the time goes in v1:
time: 57.3 us; the launch traced here: 57.1 us
  Pallas kernels  56.5 us (99%)
  between operations  0.65 us (1%)
    pallas_call x1, Pallas kernels, per_device(): pl.pallas_call(kernel, out_shape=jax.ShapeDtypeStruct((16, 384), F32), in...  54.8 us
    pallas_call x1, Pallas kernels, per_device(): pl.pallas_call(finish, out_shape=(jax.ShapeDtypeStruct((16, 384), BF16),...  1.69 us

profile of v1, /device:TPU:1, one launch (start us, length us, event | category | flops | bytes accessed | tf_op | source)
XLA Modules:
  0.0 57.1 jit_solution(10375899498248909968)
XLA Ops:
  0.6 54.8 %shard_map.203.mixed_ref = f32[16,384]{1,0:T(8,128)} custom-call(bf16[16,384]{1,0:T(8,128)(2,1)} %single_q.1, f32[12,16]{1,0:T(8,128)} %frames.1, s32[1,16]{1,0:T(1,128)} %bitcast.23, bf16[192,384]{1,0:T(8,128)(2,1)} %single_k.1, f32[12,192]{1,0:T(8,128)} %frames_k.1, s32[1,192]{1,0:T(1,128)} %bitcast.21, s32[1,192]{1,0:T(1,128)} %bitcast.22, ...), custom_call_target="tpu_custom_call" | custom-call | tf_op jit(solution)/shard_map/pallas_call | solution.py:661
  55.4 1.7 %shard_map.204 = (bf16[16,384]{1,0:T(8,128)(2,1)}, f32[12,16]{1,0:T(8,128)}) custom-call(f32[16,384]{1,0:T(8,128)} %shard_map.203.mixed_ref, f32[384]{0:T(512)} %gain.1, bf16[6,384]{1,0:T(8,128)(2,1)} %bitcast.19, f32[12,16]{1,0:T(8,128)} %frames.1), custom_call_target="tpu_custom_call" | custom-call | tf_op jit(solution)/shard_map/pallas_call | solution.py:687

commit v2 on v1

--- a/solution.py
+++ b/solution.py
@@ -23,9 +23,9 @@
     "o0": (3, 0, 1), "o1": (3, 1, 1),
 }
 SLOTS = {
-    "z0": (-1, 4, 8), "z1": (4, 6, 8), "l0": (4, 8, 8), "r0": (4, 8, 8), "z2": (-1, 8, 8), "l1": (7, 8, 8),
-    "r1": (7, 8, 8), "z3": (6, 8, 8), "l2": (5, 9, 9), "r2": (5, 9, 9), "l3": (8, 9, 9), "r3": (8, 9, 9),
-    "o0": (10, 10, 10), "o1": (11, 11, 11),
+    "z0": (-1, 3, 9), "z1": (3, 5, 9), "l0": (4, 9, 9), "r0": (4, 9, 9), "z2": (1, 8, 9), "l1": (9, 9, 9),
+    "r1": (9, 9, 9), "z3": (8, 8, 9), "l2": (11, 11, 11), "r2": (11, 11, 11), "l3": (11, 11, 11),
+    "r3": (11, 11, 11), "o0": (12, 12, 12), "o1": (13, 13, 13),
 }
 CHUNKS = 8
 KEYS = 384
@@ -217,8 +217,8 @@
     mixed_out,
     v_single, v_frames, v_chain, v_kframes, v_kchain, v_kmask, v_wq, v_wk, v_wv, v_wqp, v_wkp, v_wvp, v_wbias, v_wout,
     pairs, keys, metas, bias, pack_rows, pack_weights,
-    rows_single, rows_other, w_points, w_values, w_vpoints, factors, bias_rows,
-    acc_pair, acc_single, acc_points, top, total, part_in,
+    projections, rows_other, w_values, factors, bias_rows,
+    acc_pair, acc_single, acc_points, top, total, part_in, centers, turns,
     local_sem, pair_sem, send_sem, recv_sem,
 ):
     y = lax.axis_index("head")
@@ -236,8 +236,8 @@
 
     partner = device(lax.rem(z + jnp.where(r == 0, 1, 7), 8), x, core)
     above, below = device(lax.rem(z + 1, 8), x, core), device(lax.rem(z + 7, 8), x, core)
-    first_relay = device(lax.rem(2 * y + 3, 8), x, core)
-    second_relay = device(lax.rem(2 * y + 6, 8), x, core)
+    own_relay = device(lax.rem(2 * y + jnp.where(r == 1, 3, 6), 8), x, core)
+    other_relay = device(lax.rem(2 * y + jnp.where(r == 1, 6, 3), 8), x, core)
     right = device(z, lax.rem(x + 1, 4), core)
     left = device(z, lax.rem(x + 3, 4), core)
     sibling = device(z, x, 1 - core)
@@ -259,7 +259,7 @@
     own_copies = [
         pltpu.make_async_copy(src, dst, local_sem.at[10 + i])
         for i, (src, dst) in enumerate(
-            ((single_k, keys.at[own_index, core]), (frames_k, v_kframes), (chain_k, v_kchain), (mask_k, v_kmask))
+            ((frames_k, v_kframes), (chain_k, v_kchain), (mask_k, v_kmask), (single_k, keys.at[own_index, core]))
         )
     ]
     out_copy = pltpu.make_async_copy(w_out, v_wout, local_sem.at[14])
@@ -269,7 +269,7 @@
     ]
 
     barrier = pltpu.get_barrier_semaphore()
-    along_z = [(depth == 0, partner), (depth == 0, first_relay), (depth == 0, second_relay)]
+    along_z = [(depth == 0, partner), (depth == 0, own_relay), (depth == 0, other_relay)]
     along_z += [(depth == 1, above), (depth == 1, below)]
     along_z += [(depth == 1, device(lax.rem(2 * y, 8), x, core)), (depth == 1, device(lax.rem(2 * y + 1, 8), x, core))]
     along_z += [(depth == 2, device(lax.rem(2 * y + jnp.where(upper, 3, 6), 8), x, core))]
@@ -293,9 +293,6 @@
 
     for copy in small:
         copy.start()
-    for copy in pair_copies:
-        copy.start()
-    out_copy.start()
 
     def remote(src, dst, sent, received, target):
         return pltpu.make_async_remote_copy(
@@ -303,11 +300,11 @@
             device_id=target, device_id_type=MESH,
         )
 
-    def block(index, cc, sent, received, target, half=None, meta=True):
+    def block(index, cc, sent, received, target, half=None, meta=True, src=None):
         ref = keys.at[index, cc]
         if half is not None:
             ref = keys.at[index, cc, pl.ds(96 * half, 96)]
-        copies = [remote(ref, ref, sent, received, {"blk": target})]
+        copies = [remote(ref if src is None else src, ref, sent, received, {"blk": target})]
         if meta:
             ref = metas.at[index, cc]
             copies.append(remote(ref, ref, sent + META_OUT, received + META, {"blk": target}))
@@ -320,29 +317,37 @@
         step = 2 * phase + half
         meta = half == 0
 
-        def add(condition, sent, received, target):
-            result.append((condition, block(index, core, sent, received, target, half, meta)))
+        def add(condition, sent, received, target, at_end=True, src=None):
+            result.append((condition, block(index, core, sent, received, target, half, meta, src), at_end))
 
         if kind == 0:
             if phase == 0:
-                far = Z_IN + 2 + half
-                add(depth == 0, Z_OUT + half, far, partner)
-                add(r == 1, Z_BACK + half, Z_IN + half, first_relay)
-                add(r == 1, Z_LAST + half, far, second_relay)
-                add(r == 0, Z_BACK + half, Z_IN + half, second_relay)
-                add(r == 0, Z_LAST + half, far, first_relay)
+                own = single_k.at[pl.ds(96 * half, 96)]
+                add(depth == 0, Z_BACK + half, Z_IN + half, own_relay, False, own)
+                add(depth == 0, Z_OUT + half, Z_IN + 2 + half, partner, True, own)
+                add(depth == 0, RIGHT_OUT + step, LEFT_IN + step, right, True, own)
+                add(depth == 0, LEFT_OUT + step, RIGHT_IN + step, left, True, own)
             add(depth == 1, Z_OUT + step, Z_IN + step, above)
             add(depth == 1, Z_BACK + step, Z_IN + step, below)
-            add(None, RIGHT_OUT + step, LEFT_IN + step, right)
-            add(None, LEFT_OUT + step, RIGHT_IN + step, left)
+            passed = depth > 0 if phase == 0 else None
+            add(passed, RIGHT_OUT + step, LEFT_IN + step, right)
+            add(passed, LEFT_OUT + step, RIGHT_IN + step, left)
         if kind == 1 and half == 0:
             add(None, HALF_RIGHT_OUT + phase, HALF_LEFT_IN + phase, right)
         if kind == 2 and half == 1:
             add(None, HALF_LEFT_OUT + phase, HALF_RIGHT_IN + phase, left)
         if half == 1:
             i = chunk_of(phase, kind)
-            result.append((None, block(index, core, CORE_OUT + i, CORE_IN + i, sibling)))
+            result.append((None, block(index, core, CORE_OUT + i, CORE_IN + i, sibling), True))
         return result
+
+    def near_copies(half):
+        own = single_k.at[pl.ds(96 * half, 96)]
+        return block(own_index, core, Z_BACK + half, Z_IN + half, own_relay, half, half == 0, own)
+
+    def far_copies(half):
+        own = single_k.at[pl.ds(96 * half, 96)]
+        return block(own_index, core, Z_LAST + half, Z_IN + 2 + half, other_relay, half, half == 0, own)
 
     def run(condition, copies, verb):
         def act():
@@ -365,7 +370,7 @@
             place = (Z_IN, LEFT_IN, RIGHT_IN)[kind] + step
             arriving = block(index, core, 0, place, sibling, half, half == 0)
         run(depth > 0 if kind == 0 and phase == 0 else None, arriving, "wait_recv")
-        for condition, copies in sends(name):
+        for condition, copies, _ in sends(name):
             run(condition, copies, "start")
 
     slots = {
@@ -376,17 +381,25 @@
         for name in names:
             pl.when(slots[name] == step)(lambda name=name: event(name))
 
+    pl.semaphore_wait(barrier, jnp.where(depth == 0, 9, jnp.where(depth == 1, 10, 7)))
+    first = [copies for condition, copies, _ in sends("z0") if condition is not None][:4]
+
     @pl.when(depth == 0)
     def _():
-        for copy in own_copies:
+        for copies in first:
+            copies[0].start()
+        for copy in own_copies[:3]:
             copy.wait()
         metas[own_index, core] = jnp.zeros((16, 256), F32)
         metas[own_index, core, :12, :192] = v_kframes[...]
         metas[own_index, core, 12:13, :192] = v_kchain[...].astype(F32)
         metas[own_index, core, 13:14, :192] = v_kmask[...].astype(F32)
-
-    pl.semaphore_wait(barrier, jnp.where(depth == 0, 9, jnp.where(depth == 1, 10, 7)))
-    events_at(-1, ["z0", "z2"])
+        for copies in first:
+            copies[1].start()
+
+    for copy in pair_copies:
+        copy.start()
+    out_copy.start()
 
     for copy in small:
         copy.wait()
@@ -418,6 +431,19 @@
     for copy in rows_sent + weights_sent:
         copy.start()
 
+    row = iota((ROWS, 16), 0)
+    frames = nt(ones_where(by12(row) == iota((ROWS, 16), 1), F32), v_frames[...], HIGH)
+    centers[...] = frames[:, 9:12]
+    lane = iota((1, 128), 1)
+    axis = (lane - 16) >> 3
+    inside = (lane >= 16) & (lane < 40)
+    entry = iota((12, 128), 0)
+    for b in range(3):
+        turns[b] = mm(frames, ones_where((entry == 3 * b + axis) & inside, F32), HIGH)
+
+    run(depth == 0, near_copies(0), "wait_send")
+    run(depth == 0, far_copies(0), "start")
+
     col = iota((32, 12), 1)
     pick_row = iota((32, 12), 0)
     first = mm(ones_where(pick_row == col), v_wbias[...])
@@ -434,30 +460,35 @@
             out = short(out) * WEIGHT_L
             bias[c, t] = out[:, :KEYS]
             bias[c + 1, t] = out[:, KEYS:]
+        run((depth == 0) & (t == 1), far_copies(0), "wait_send")
+        run((depth == 0) & (t == 3), near_copies(1), "wait_send")
+        run((depth == 0) & (t == 3), far_copies(1), "start")
+        run((depth == 0) & (t == 1), own_copies[3:], "wait")
         events_at(t, [name for name, when in SLOTS.items() if any(0 <= k < 8 for k in when)])
         return 0
 
     lax.fori_loop(0, GROUPS, bias_step, 0)
-    events_at(8, [name for name, when in SLOTS.items() if 8 in when])
+    events_at(8, ["z2", "z3"])
+    events_at(9, [name for name, when in SLOTS.items() if 9 in when])
 
     for copy in rows_arriving + weights_arriving:
         copy.wait_recv()
     for_single, for_other, factor = all_rows(pack_rows[...].reshape(ROWS, 512))
-    rows_single[...] = for_single
+    projections[:ROWS] = for_single
     rows_other[...] = for_other
     factors[...] = -factor
     packs = pack_weights[...]
     row, col = iota((ROWS, ROWS), 0), iota((ROWS, ROWS), 1)
     place = row & 15
     pick = col == (place >> 2) * 48 + (row >> 6) * 16 + ((row >> 4) & 3) * 4 + (place & 3)
-    w_points[...] = mm(ones_where(pick), packs[:, :48].reshape(ROWS, 384)).astype(BF16)
+    projections[ROWS : 2 * ROWS] = mm(ones_where(pick), packs[:, :48].reshape(ROWS, 384)).astype(BF16)
     w_values[...] = packs[:, 48:96].reshape(ROWS, 384)
     row, col = iota((288, 320), 0), iota((288, 320), 1)
     b = by96(row)
     rest = row - b * 96
     owner = by24(rest)
     pick = col == owner * 80 + b * 24 + rest - owner * 24
-    w_vpoints[...] = mm(ones_where(pick), packs[:, 96:].reshape(320, 384)).astype(BF16)
+    projections[2 * ROWS :] = mm(ones_where(pick), packs[:, 96:].reshape(320, 384)).astype(BF16)
 
     acc_pair[...] = jnp.zeros_like(acc_pair)
     acc_single[...] = jnp.zeros_like(acc_single)
@@ -481,7 +512,7 @@
         return [first[:, :128], jnp.where(half, first[:, 128:], start), jnp.where(half, start, end)]
 
     def key_step(s, _):
-        events_at(jnp.where(s == 0, -2, s + 8), [name for name, when in SLOTS.items() if max(when) > 8])
+        events_at(s + 10, [name for name, when in SLOTS.items() if max(when) > 9])
         pair_of = []
         for k in range(2):
             i = 2 * s + k
@@ -504,7 +535,8 @@
                 result.append(moved.astype(BF16))
             return result
 
-        points = placed(nt(w_points[...], single), 64)
+        projected = nt(projections[...], single)
+        points = placed(projected[ROWS : 2 * ROWS], 64)
         square = 0.0
         for part in points:
             wide = part.astype(F32)
@@ -516,7 +548,7 @@
         others = jnp.concatenate(
             points + points + [chains, chains] + norms + [jnp.full((16, width), 1.0, BF16)], axis=0
         )
-        logit = nt(rows_single[...], single) + mm(rows_other[...], others)
+        logit = projected[:ROWS] + mm(rows_other[...], others)
         logit = logit + jnp.concatenate([bias[index].reshape(ROWS, KEYS) for index in pair_of], axis=1)
         logit = jnp.where(meta[13:14] > 0.5, logit, -1000000000.0)
         old = top[...]
@@ -527,7 +559,7 @@
         total[...] = total[...] * scale + jnp.sum(weight, axis=1, keepdims=True)
         weight_b = weight.astype(BF16)
         acc_single[...] = acc_single[...] * scale + mm(weight_b, single)
-        vpoints = jnp.concatenate(placed(nt(w_vpoints[...], single), 96), axis=0)
+        vpoints = jnp.concatenate(placed(projected[2 * ROWS :], 96), axis=0)
         acc_points[...] = acc_points[...] * scale + nt(weight_b, vpoints)
         upper_rows = iota((GROUP, 128), 0) < 12
         for g in range(GROUPS):
@@ -558,10 +590,10 @@
     again = lane & 63
     source = iota((ROWS, 128), 0)
     other = mm(scalar, ones_where(((source & 15) == again) & (again < 16)))
-    frames = nt(ones_where(query == iota((ROWS, 16), 1), F32), v_frames[...], HIGH)
+    center = centers[...]
     col = iota((1, 288), 1)
     axis = by96(col)
-    center = jnp.where(axis == 0, frames[:, 9:10], jnp.where(axis == 1, frames[:, 10:11], frames[:, 11:12]))
+    center = jnp.where(axis == 0, center[:, :1], jnp.where(axis == 1, center[:, 1:2], center[:, 2:3]))
     shifted = jnp.where(((col - axis * 96) >> 3) == head, acc_points[...] * inverse - center, 0.0).astype(BF16)
     source = iota((288, 128), 0)
     other = other + mm(shifted, ones_where(again == by96(source) * 8 + (source & 7) + 16))
@@ -592,18 +624,18 @@
     o_pair = sum(p * s for p, s in zip(pair_parts, shares)).astype(BF16)
     other = sum(p * s for p, s in zip(others, shares))
     inside = (lane >= 16) & (lane < 40)
-    axis = (lane - 16) >> 3
     point = lane & 7
     source = iota((128, 128), 0)
-    entry = iota((12, 128), 0)
+    first, second = split2(other)
     located = 0.0
     for b in range(3):
-        pick = (source == point + 16 + 8 * b) & inside
-        turn = mm(frames, ones_where((entry == 3 * b + axis) & inside, F32), HIGH)
-        located = located + turn * mm(other, ones_where(pick, F32), HIGH)
+        pick = ones_where((source == point + 16 + 8 * b) & inside)
+        located = located + turns[b] * (mm(first.astype(BF16), pick) + mm(second.astype(BF16), pick))
     last = (lane >= 40) & (lane < 48)
     pick = (source >= 16) & (source < 40) & ((source & 7) == point) & last
-    length = jnp.sqrt(mm(located * located, ones_where(pick, F32), HIGH) + 1e-08)
+    first, second = split2(located * located)
+    pick = ones_where(pick)
+    length = jnp.sqrt(mm(first.astype(BF16), pick) + mm(second.astype(BF16), pick) + 1e-08)
     feats = jnp.where(lane < 16, other, jnp.where(inside, located, jnp.where(last, length, 0.0)))
     feats = jnp.concatenate([o_pair, feats.astype(BF16)], axis=1)
     row, col = iota((ROWS, ROWS), 0), iota((ROWS, ROWS), 1)
@@ -621,8 +653,10 @@
     mixed_out[...] = update
 
     for name in EVENTS:
-        for condition, copies in sends(name):
-            run(condition, copies, "wait_send")
+        for condition, copies, at_end in sends(name):
+            if at_end:
+                run(condition, copies, "wait_send")
+    run(depth == 0, far_copies(1), "wait_send")
     for copy in rows_sent + weights_sent + parts_sent:
         copy.wait_send()
 
@@ -670,10 +704,11 @@
             vm((12, 128), BF16), vm((2112, 384), BF16),
             vm((16, CHUNKS, KEYS, 128), BF16), vm((CHUNKS, 2, 192, 384), BF16), vm((CHUNKS, 2, 16, 256), F32),
             vm((CHUNKS, GROUPS, GROUP, KEYS), F32), vm((4, 48, 512), BF16), vm((4, 176, 384), BF16),
-            vm((ROWS, 384), BF16), vm((ROWS, 512), BF16), vm((ROWS, 384), BF16), vm((ROWS, 384), BF16),
-            vm((288, 384), BF16), vm((16, 1), F32), vm((32, 256), BF16),
+            vm((2 * ROWS + 288, 384), BF16), vm((ROWS, 512), BF16), vm((ROWS, 384), BF16), vm((16, 1), F32),
+            vm((32, 256), BF16),
             vm((GROUPS, GROUP, 128), F32), vm((ROWS, 384), F32), vm((ROWS, 288), F32),
             vm((ROWS, 1), F32), vm((ROWS, 1), F32), vm((4, 288, 128), BF16),
+            vm((ROWS, 3), F32), vm((3, ROWS, 128), F32),
             pltpu.SemaphoreType.DMA((15,)), pltpu.SemaphoreType.DMA((GROUPS,)),
             pltpu.SemaphoreType.DMA((80,)), pltpu.SemaphoreType.DMA((64,)),
         ],

time: 57.3 us -> 54.4 us (0.949)
  Pallas kernels: 56.5 us -> 53.6 us
    pallas_call x1, Pallas kernels: 54.8 us -> 51.9 us  [per_device(): pl.pallas_call(kernel, out_shape=jax.ShapeDtypeStruct((16, 384), F32), in...]
where the time goes in v2:
time: 54.4 us; the launch traced here: 54.2 us
  Pallas kernels  53.6 us (99%)
  between operations  0.65 us (1%)
    pallas_call x1, Pallas kernels, per_device(): pl.pallas_call(kernel, out_shape=jax.ShapeDtypeStruct((16, 384), F32), in...  51.9 us
    pallas_call x1, Pallas kernels, per_device(): pl.pallas_call(finish, out_shape=(jax.ShapeDtypeStruct((16, 384), BF16),...  1.69 us

profile of v2, /device:TPU:1, one launch (start us, length us, event | category | flops | bytes accessed | tf_op | source)
XLA Modules:
  0.0 54.2 jit_solution(14159163101393989281)
XLA Ops:
  0.6 51.9 %shard_map.203.mixed_ref = f32[16,384]{1,0:T(8,128)} custom-call(bf16[16,384]{1,0:T(8,128)(2,1)} %single_q.1, f32[12,16]{1,0:T(8,128)} %frames.1, s32[1,16]{1,0:T(1,128)} %bitcast.23, bf16[192,384]{1,0:T(8,128)(2,1)} %single_k.1, f32[12,192]{1,0:T(8,128)} %frames_k.1, s32[1,192]{1,0:T(1,128)} %bitcast.21, s32[1,192]{1,0:T(1,128)} %bitcast.22, ...), custom_call_target="tpu_custom_call" | custom-call | tf_op jit(solution)/shard_map/pallas_call | solution.py:695
  52.5 1.7 %shard_map.204 = (bf16[16,384]{1,0:T(8,128)(2,1)}, f32[12,16]{1,0:T(8,128)}) custom-call(f32[16,384]{1,0:T(8,128)} %shard_map.203.mixed_ref, f32[384]{0:T(512)} %gain.1, bf16[6,384]{1,0:T(8,128)(2,1)} %bitcast.19, f32[12,16]{1,0:T(8,128)} %frames.1), custom_call_target="tpu_custom_call" | custom-call | tf_op jit(solution)/shard_map/pallas_call | solution.py:722

commit v3 on v2

--- a/solution.py
+++ b/solution.py
@@ -511,13 +511,10 @@
         end = pltpu.roll(second[:, 128:], 64, 1)
         return [first[:, :128], jnp.where(half, first[:, 128:], start), jnp.where(half, start, end)]
 
-    def key_step(s, _):
-        events_at(s + 10, [name for name, when in SLOTS.items() if max(when) > 9])
-        pair_of = []
-        for k in range(2):
+    def front(s):
+        pair_of = [index_of(2 * s), index_of(2 * s + 1)]
+        for k, index in enumerate(pair_of):
             i = 2 * s + k
-            index = index_of(i)
-            pair_of.append(index)
             here = keys.at[index, 1 - core]
             remote(here, here, 0, CORE_IN + i, {"blk": sibling}).wait_recv()
             here = metas.at[index, 1 - core]
@@ -551,6 +548,12 @@
         logit = projected[:ROWS] + mm(rows_other[...], others)
         logit = logit + jnp.concatenate([bias[index].reshape(ROWS, KEYS) for index in pair_of], axis=1)
         logit = jnp.where(meta[13:14] > 0.5, logit, -1000000000.0)
+        vpoints = jnp.concatenate(placed(projected[2 * ROWS :], 96), axis=0)
+        return logit, vpoints
+
+    def back(s, logit, vpoints):
+        pair_of = [index_of(2 * s), index_of(2 * s + 1)]
+        single = jnp.concatenate([keys[index].reshape(KEYS, 384) for index in pair_of], axis=0)
         old = top[...]
         new = jnp.maximum(old, jnp.max(logit, axis=1, keepdims=True))
         scale = jnp.exp(old - new)
@@ -559,7 +562,6 @@
         total[...] = total[...] * scale + jnp.sum(weight, axis=1, keepdims=True)
         weight_b = weight.astype(BF16)
         acc_single[...] = acc_single[...] * scale + mm(weight_b, single)
-        vpoints = jnp.concatenate(placed(projected[2 * ROWS :], 96), axis=0)
         acc_points[...] = acc_points[...] * scale + nt(weight_b, vpoints)
         upper_rows = iota((GROUP, 128), 0) < 12
         for g in range(GROUPS):
@@ -574,9 +576,14 @@
             out = mm(weight[lo : lo + GROUP].astype(BF16), there)
             out = jnp.where(upper_rows, out[:, :128], out[:, 128:])
             acc_pair[g] = acc_pair[g] * scale[lo : lo + GROUP] + out
-        return 0
-
-    lax.fori_loop(0, 4, key_step, 0)
+
+    def key_step(s, before):
+        events_at(s + 10, [name for name, when in SLOTS.items() if max(when) > 9])
+        after = front(s)
+        back(s - 1, *before)
+        return after
+
+    back(3, *lax.fori_loop(1, 4, key_step, front(0)))
 
     inverse = 1.0 / total[...]
     row = iota((ROWS, 1), 0)

time: 54.4 us -> 53.6 us (0.985)
  Pallas kernels: 53.6 us -> 52.8 us
    pallas_call x1, Pallas kernels: 51.9 us -> 51.1 us  [per_device(): pl.pallas_call(kernel, out_shape=jax.ShapeDtypeStruct((16, 384), F32), in...]
where the time goes in v3:
time: 53.6 us; the launch traced here: 53.4 us
  Pallas kernels  52.8 us (99%)
  between operations  0.65 us (1%)
    pallas_call x1, Pallas kernels, per_device(): pl.pallas_call(kernel, out_shape=jax.ShapeDtypeStruct((16, 384), F32), in...  51.1 us
    pallas_call x1, Pallas kernels, per_device(): pl.pallas_call(finish, out_shape=(jax.ShapeDtypeStruct((16, 384), BF16),...  1.69 us

profile of v3, /device:TPU:1, one launch (start us, length us, event | category | flops | bytes accessed | tf_op | source)
XLA Modules:
  0.0 53.4 jit_solution(10329093170516351987)
XLA Ops:
  0.6 51.1 %shard_map.203.mixed_ref = f32[16,384]{1,0:T(8,128)} custom-call(bf16[16,384]{1,0:T(8,128)(2,1)} %single_q.1, f32[12,16]{1,0:T(8,128)} %frames.1, s32[1,16]{1,0:T(1,128)} %bitcast.23, bf16[192,384]{1,0:T(8,128)(2,1)} %single_k.1, f32[12,192]{1,0:T(8,128)} %frames_k.1, s32[1,192]{1,0:T(1,128)} %bitcast.21, s32[1,192]{1,0:T(1,128)} %bitcast.22, ...), custom_call_target="tpu_custom_call" | custom-call | tf_op jit(solution)/shard_map/pallas_call | solution.py:702
  51.7 1.7 %shard_map.204 = (bf16[16,384]{1,0:T(8,128)(2,1)}, f32[12,16]{1,0:T(8,128)}) custom-call(f32[16,384]{1,0:T(8,128)} %shard_map.203.mixed_ref, f32[384]{0:T(512)} %gain.1, bf16[6,384]{1,0:T(8,128)(2,1)} %bitcast.19, f32[12,16]{1,0:T(8,128)} %frames.1), custom_call_target="tpu_custom_call" | custom-call | tf_op jit(solution)/shard_map/pallas_call | solution.py:729

commit v4 on v3

--- a/solution.py
+++ b/solution.py
@@ -33,9 +33,9 @@
 WEIGHT_C = math.sqrt(2.0 / (9.0 * QPTS))
 
 Z_IN, LEFT_IN, RIGHT_IN, HALF_LEFT_IN, HALF_RIGHT_IN, CORE_IN = 0, 4, 8, 12, 14, 16
-ROWS_IN, WEIGHTS_IN, PART_IN, META = 24, 27, 30, 33
+ROWS_IN, WEIGHTS_IN, PART_IN, META, REST_IN = 24, 27, 30, 33, 57
 Z_OUT, Z_BACK, Z_LAST, RIGHT_OUT, LEFT_OUT, HALF_RIGHT_OUT, HALF_LEFT_OUT, CORE_OUT = 0, 4, 8, 12, 16, 20, 22, 24
-ROWS_OUT, WEIGHTS_OUT, PART_OUT, META_OUT = 32, 35, 38, 41
+ROWS_OUT, WEIGHTS_OUT, PART_OUT, META_OUT, REST_OUT = 32, 35, 38, 41, 74
 
 
 def iota(shape, dim):
@@ -218,7 +218,7 @@
     v_single, v_frames, v_chain, v_kframes, v_kchain, v_kmask, v_wq, v_wk, v_wv, v_wqp, v_wkp, v_wvp, v_wbias, v_wout,
     pairs, keys, metas, bias, pack_rows, pack_weights,
     projections, rows_other, w_values, factors, bias_rows,
-    acc_pair, acc_single, acc_points, top, total, part_in, centers, turns,
+    acc_pair, acc_single, acc_points, top, total, part_in, rest_in, centers, turns,
     local_sem, pair_sem, send_sem, recv_sem,
 ):
     y = lax.axis_index("head")
@@ -589,7 +589,10 @@
     row = iota((ROWS, 1), 0)
     query = by12(row)
     head = row - query * 12
-    part_in[y, :ROWS] = (acc_pair[...].reshape(ROWS, 128) * inverse).astype(BF16)
+    part_in[y] = (acc_pair[...].reshape(ROWS, 128) * inverse).astype(BF16)
+    parts_sent, parts_arriving = exchange(lambda peer: part_in.at[y], part_in, PART_OUT, PART_IN)
+    for copy in parts_sent:
+        copy.start()
     hi, lo = split2(acc_single[...] * inverse)
     scalar = nt(hi.astype(BF16), w_values[...]) + nt(lo.astype(BF16), w_values[...])
     scalar = jnp.where((iota((ROWS, ROWS), 1) >> 4) == head, scalar, 0.0).astype(BF16)
@@ -608,18 +611,18 @@
         for step, piece in enumerate(split3(value)):
             other = jnp.where(again == start + step, piece, other)
     half = ROWS // 2
-    part_in[y, ROWS:] = jnp.where(lane < 64, other[:half], other[half:]).astype(BF16)
-
-    parts_sent, parts_arriving = exchange(lambda peer: part_in.at[y], part_in, PART_OUT, PART_IN)
-    for copy in parts_sent:
+    rest_in[y] = jnp.where(lane < 64, other[:half], other[half:]).astype(BF16)
+
+    rest_sent, rest_arriving = exchange(lambda peer: rest_in.at[y], rest_in, REST_OUT, REST_IN)
+    for copy in rest_sent:
         copy.start()
-    for copy in parts_arriving:
+    for copy in parts_arriving + rest_arriving:
         copy.wait_recv()
 
-    pair_parts = [part_in[k, :ROWS].astype(F32) for k in range(4)]
+    pair_parts = [part_in[k].astype(F32) for k in range(4)]
     others = []
     for k in range(4):
-        both = part_in[k, ROWS:].astype(F32)
+        both = rest_in[k].astype(F32)
         others.append(jnp.concatenate([both, pltpu.roll(both, 64, 1)], axis=0))
     tops = [p[:, 40:41] + p[:, 41:42] + p[:, 42:43] for p in others]
     best = jnp.maximum(jnp.maximum(tops[0], tops[1]), jnp.maximum(tops[2], tops[3]))
@@ -664,7 +667,7 @@
             if at_end:
                 run(condition, copies, "wait_send")
     run(depth == 0, far_copies(1), "wait_send")
-    for copy in rows_sent + weights_sent + parts_sent:
+    for copy in rows_sent + weights_sent + parts_sent + rest_sent:
         copy.wait_send()
 
 
@@ -714,7 +717,7 @@
             vm((2 * ROWS + 288, 384), BF16), vm((ROWS, 512), BF16), vm((ROWS, 384), BF16), vm((16, 1), F32),
             vm((32, 256), BF16),
             vm((GROUPS, GROUP, 128), F32), vm((ROWS, 384), F32), vm((ROWS, 288), F32),
-            vm((ROWS, 1), F32), vm((ROWS, 1), F32), vm((4, 288, 128), BF16),
+            vm((ROWS, 1), F32), vm((ROWS, 1), F32), vm((4, ROWS, 128), BF16), vm((4, ROWS // 2, 128), BF16),
             vm((ROWS, 3), F32), vm((3, ROWS, 128), F32),
             pltpu.SemaphoreType.DMA((15,)), pltpu.SemaphoreType.DMA((GROUPS,)),
             pltpu.SemaphoreType.DMA((80,)), pltpu.SemaphoreType.DMA((64,)),

time: 53.6 us -> 53.2 us (level)
  no operation moved by 1% of the time
where the time goes in v4:
time: 53.2 us; the launch traced here: 53 us
  Pallas kernels  52.4 us (98%)
  between operations  0.65 us (1%)
    pallas_call x1, Pallas kernels, per_device(): pl.pallas_call(kernel, out_shape=jax.ShapeDtypeStruct((16, 384), F32), in...  50.7 us
    pallas_call x1, Pallas kernels, per_device(): pl.pallas_call(finish, out_shape=(jax.ShapeDtypeStruct((16, 384), BF16),...  1.69 us

profile of v4, /device:TPU:1, one launch (start us, length us, event | category | flops | bytes accessed | tf_op | source)
XLA Modules:
  0.0 53.0 jit_solution(11667871308544928335)
XLA Ops:
  0.6 50.7 %shard_map.203.mixed_ref = f32[16,384]{1,0:T(8,128)} custom-call(bf16[16,384]{1,0:T(8,128)(2,1)} %single_q.1, f32[12,16]{1,0:T(8,128)} %frames.1, s32[1,16]{1,0:T(1,128)} %bitcast.23, bf16[192,384]{1,0:T(8,128)(2,1)} %single_k.1, f32[12,192]{1,0:T(8,128)} %frames_k.1, s32[1,192]{1,0:T(1,128)} %bitcast.21, s32[1,192]{1,0:T(1,128)} %bitcast.22, ...), custom_call_target="tpu_custom_call" | custom-call | tf_op jit(solution)/shard_map/pallas_call | solution.py:705
  51.3 1.7 %shard_map.204 = (bf16[16,384]{1,0:T(8,128)(2,1)}, f32[12,16]{1,0:T(8,128)}) custom-call(f32[16,384]{1,0:T(8,128)} %shard_map.203.mixed_ref, f32[384]{0:T(512)} %gain.1, bf16[6,384]{1,0:T(8,128)(2,1)} %bitcast.19, f32[12,16]{1,0:T(8,128)} %frames.1), custom_call_target="tpu_custom_call" | custom-call | tf_op jit(solution)/shard_map/pallas_call | solution.py:732
